TPU v7x, 512 devices: a whole 4x8x8 slice. The times are simulated.
512 devices in a mesh: ctx: 64 (over y_lo, z, core), mp: 8 (over x, y_hi).
Axes of the slice: x: 4, y: 8 (y_hi: 2, y_lo: 4; y = y_hi * 4 + y_lo), z: 8, core: 2. Of those that a mesh axis runs over, the one named last changes fastest.
Arguments:
- queries: bfloat16 [16384, 5120], P('ctx', 'mp'), may hold values from -10 to 10
- keys: bfloat16 [16384, 1024], P('ctx', 'mp'), may hold values from -20 to 20
- values: bfloat16 [16384, 1024], P('ctx', 'mp'), may hold values from -6 to 6
- kept_rows: int32 [64, 8, 128], P('ctx', 'mp'), may hold values from 0 to 255, as said below
- out_weight: bfloat16 [5120, 3072], P('ctx', 'mp'), may hold values from -0.8984375 to 0.8984375
Outputs:
- projected: bfloat16 [16384, 3072], P('ctx', 'mp')
Inputs may be any that keep to these rules, and one draw needn't show every extreme that they name: Each list kept_rows[b, g] holds 128 distinct row numbers of its block, in rising order.
All inputs are finite; a program needn't handle non-finite values.
Results may differ from a plain program's by a relative error of at most 0.011.
Values may be sent and summed in bfloat16 or wider, within the bound.
No kernel may reach another device: no remote copies, remote signals or barrier semaphores. Data moves between devices by JAX's collectives and lax.ppermute only.
A program may use at most 64 MiB of HBM per device.

v0:
```python
import jax
import jax.numpy as jnp
from jax import lax
from jax.sharding import PartitionSpec as P

QH = 40
KV = 8
HD = 128
ANCHOR = 128
PASS = 128


masked_score = -1e30


def spread(value, axis, source):
    kept = jnp.where(lax.axis_index(axis) == source, value, 0).astype(value.dtype)
    return lax.psum(kept, axis)


def shifted(block, axis, distance):
    devices = range(lax.axis_size(axis))
    route = [(i - distance, i) for i in devices if i - distance in devices]
    return lax.ppermute(block, axis, route)


def block_scores(grouped, key_block, heads_kv):
    key_split = key_block.reshape(key_block.shape[0], heads_kv, HD)
    return jnp.einsum(
        "rhgd,khd->hgrk", grouped, key_split, preferred_element_type=jnp.float32
    ) * HD ** (-0.5)


def block_values(weights, value_block, heads_kv):
    value_split = value_block.reshape(value_block.shape[0], heads_kv, HD)
    return jnp.einsum(
        "hgrk,khd->hgrd",
        weights.astype(jnp.bfloat16),
        value_split,
        preferred_element_type=jnp.float32,
    )


def absorb(running, grouped, key_block, value_block, usable, heads_kv):
    row_max, denominator, summed = running
    scores = jnp.where(
        usable[None, None, None, :], block_scores(grouped, key_block, heads_kv), masked_score
    )
    new_max = jnp.maximum(row_max, jnp.max(scores, axis=-1))
    rescale = jnp.exp(row_max - new_max)
    weights = jnp.exp(scores - new_max[..., None])
    denominator = denominator * rescale + jnp.sum(weights, axis=-1)
    summed = summed * rescale[..., None] + block_values(weights, value_block, heads_kv)
    return (new_max, denominator, summed)


def local(queries, keys, values, kept_rows, out_weight):
    row_count = queries.shape[0]
    heads_kv = keys.shape[1] // HD
    group = QH // KV
    host_idx = lax.axis_index("ctx")
    hosts = lax.axis_size("ctx")
    grouped = queries.reshape(row_count, heads_kv, group, HD)
    anchor_keys, anchor_vals = (spread(keys[:ANCHOR], "ctx", 0), spread(values[:ANCHOR], "ctx", 0))
    first_keys = jnp.concatenate([anchor_keys, keys], 0)
    first_vals = jnp.concatenate([anchor_vals, values], 0)
    positions = jnp.arange(row_count, dtype=jnp.int32)
    visible = jnp.concatenate(
        [
            jnp.broadcast_to(host_idx > 0, (row_count, ANCHOR)),
            positions[:, None] >= positions[None, :],
        ],
        1,
    )
    scores = jnp.where(
        visible[None, None], block_scores(grouped, first_keys, heads_kv), masked_score
    )
    row_max = jnp.max(scores, axis=-1)
    weights = jnp.exp(scores - row_max[..., None])
    running = (row_max, jnp.sum(weights, axis=-1), block_values(weights, first_vals, heads_kv))
    picker = jnp.transpose(kept_rows[0], (1, 0))[:, :, None]
    kept_keys = jnp.take_along_axis(keys.reshape(row_count, heads_kv, HD), picker, axis=0).reshape(
        PASS, heads_kv * HD
    )
    kept_vals = jnp.take_along_axis(
        values.reshape(row_count, heads_kv, HD), picker, axis=0
    ).reshape(PASS, heads_kv * HD)
    all_usable = jnp.ones((PASS,), dtype=bool)

    def visit(stop_idx, carry):
        held, moving_keys, moving_vals = carry
        moving_keys, moving_vals = shifted((moving_keys, moving_vals), "ctx", 1)
        held = lax.cond(
            stop_idx <= host_idx,
            lambda inner: absorb(inner, grouped, moving_keys, moving_vals, all_usable, heads_kv),
            lambda inner: inner,
            held,
        )
        return (held, moving_keys, moving_vals)

    running, _, _ = lax.fori_loop(1, hosts, visit, (running, kept_keys, kept_vals))
    row_max, denominator, summed = running
    attended = (summed / denominator[..., None]).astype(jnp.bfloat16)
    attended = jnp.transpose(attended, (2, 0, 1, 3)).reshape(row_count, heads_kv * group * HD)
    every_head = lax.all_gather(attended, "mp", axis=1, tiled=True)
    projected = jnp.dot(
        every_head,
        lax.all_gather(out_weight, "ctx", axis=0, tiled=True),
        preferred_element_type=jnp.float32,
    )
    return projected.astype(jnp.bfloat16)


def solution(mesh):
    placed = (P("ctx", "mp"), P("ctx", "mp"), P("ctx", "mp"), P("ctx", "mp", None), P("ctx", "mp"))
    return jax.shard_map(
        local, mesh=mesh, in_specs=placed, out_specs=P("ctx", "mp"), check_vma=False
    )
```

profile of v0, /device:TPU:1, one launch (start us, length us, event | category | flops | bytes accessed | tf_op | source)
XLA Modules:
  0.0 1306.3 jit_solution(6747334394104327203)
XLA Ops:
  13.9 463.5 %all-reduce.4.cloned.1.call-done = (bf16[128,128]{1,0:T(8,128)(2,1)}, bf16[128,128]{1,0:T(8,128)(2,1)}) async-done(((bf16[128,128]{1,0:T(8,128)(2,1)}, bf16[128,128]{1,0:T(8,128)(2,1)}), (bf16[128,128]{1,0:T(8,128)(2,1)}, bf16[128,128]{1,0:T(8,128)(2,1)})) %all-reduce.4.cloned.1.call-update) | async-done | bytes 65552 | tf_op jit(solution)/shard_map/psum | solution.py:18
  479.5 545.3 %while.21 = (s32[]{:T(128)}, f32[1,5,256]{2,1,0:T(8,128)S(1)}, f32[1,5,256]{2,1,0:T(8,128)S(1)}, f32[1,5,256,128]{3,2,1,0:T(8,128)S(1)}, bf16[128,128]{1,0:T(8,1...) while((s32[]{:T(128)}, f32[1,5,256]{2,1,0:T(8,128)S(1)}, ...), condition=%wide.region_9.11_spmd, body=%wide.region_4.10_spmd.sunk | while | flops 85200640 | bytes 4145443 | solution.py:101
  479.5 4.9 collective-permute-start
  495.8 5.1 collective-permute-start
  569.4 4.8 collective-permute-start
  577.8 4.8 collective-permute-start
  586.2 4.8 collective-permute-start
  594.6 4.8 collective-permute-start
  611.4 4.8 collective-permute-start
  619.8 4.8 collective-permute-start
  636.6 4.8 collective-permute-start
  645.0 4.8 collective-permute-start
  670.2 4.8 collective-permute-start
  695.4 4.8 collective-permute-start
  720.6 4.8 collective-permute-start
  745.8 5.0 collective-permute-start
  755.1 5.0 collective-permute-start
  764.4 5.0 collective-permute-start
  773.7 5.0 collective-permute-start
  783.0 5.0 collective-permute-start
  792.3 5.0 collective-permute-start
  801.6 5.0 collective-permute-start
  810.9 5.0 collective-permute-start
  820.2 5.0 collective-permute-start
  829.5 5.0 collective-permute-start
  838.8 5.0 collective-permute-start
  848.1 5.0 collective-permute-start
  857.4 5.0 collective-permute-start
  866.7 5.0 collective-permute-start
  876.0 5.0 collective-permute-start
  885.3 5.0 collective-permute-start
  894.6 5.0 collective-permute-start
  903.9 5.0 collective-permute-start
  913.2 5.0 collective-permute-start
  922.5 5.0 collective-permute-start
  931.8 5.0 collective-permute-start
  941.1 5.0 collective-permute-start
  950.4 5.0 collective-permute-start
  959.7 5.0 collective-permute-start
  969.0 5.0 collective-permute-start
  978.3 5.0 collective-permute-start
  987.6 5.0 collective-permute-start
  996.9 5.0 collective-permute-start
  1006.2 5.0 collective-permute-start
  1015.5 5.0 collective-permute-start
  1026.5 144.1 %all-gather.3.cloned.1.call-done = bf16[256,5120]{0,1:T(8,128)(2,1)} async-done(((bf16[256,640]{0,1:T(8,128)(2,1)}), bf16[256,5120]{0,1:T(8,128)(2,1)}) %all-gather.3.cloned.1.call-update) | async-done | bytes 2621456 | tf_op jit(solution)/shard_map/all_gather | solution.py:105
  1170.6 124.0 %all-gather.5.cloned.1.call-done = bf16[5120,384]{1,0:T(8,128)(2,1)} async-done(((bf16[80,384]{1,0:T(8,128)(2,1)}), bf16[5120,384]{1,0:T(8,128)(2,1)}) %all-gather.5.cloned.1.call-update) | async-done | bytes 3932176 | tf_op jit(solution)/shard_map/all_gather | solution.py:108
  1294.6 5.2 convolution_convert_fusion
  (432 shorter events, 342.5 us)
Async XLA Ops:
  6.5 470.9 %all-reduce.4.cloned.1.call-start = ((), (), s32[]{:S(2)}) async-start(), calls=%async_computation.2 | async-start | bytes 131072 | tf_op jit(solution)/shard_map/psum | solution.py:18
  8.0 1162.6 %all-gather.3.cloned.1.call-start = ((), (), s32[]{:S(2)}) async-start(), calls=%async_computation | async-start | bytes 2949120 | tf_op jit(solution)/shard_map/all_gather | solution.py:105
  569.4 7.4 collective-permute-start
  577.8 7.4 collective-permute-start
  586.2 7.4 collective-permute-start
  594.6 7.4 collective-permute-start
  603.0 7.4 collective-permute-start
  611.4 7.4 collective-permute-start
  619.8 7.4 collective-permute-start
  628.2 7.4 collective-permute-start
  636.6 7.4 collective-permute-start
  645.0 7.4 collective-permute-start
  653.4 7.4 collective-permute-start
  661.8 7.4 collective-permute-start
  670.2 7.4 collective-permute-start
  695.4 7.4 collective-permute-start
  720.6 7.4 collective-permute-start
  745.8 8.3 collective-permute-start
  755.1 8.3 collective-permute-start
  764.4 8.3 collective-permute-start
  773.7 8.3 collective-permute-start
  783.0 8.3 collective-permute-start
  792.3 8.3 collective-permute-start
  801.6 8.3 collective-permute-start
  810.9 8.3 collective-permute-start
  820.2 8.3 collective-permute-start
  829.5 8.3 collective-permute-start
  838.8 8.3 collective-permute-start
  848.1 8.3 collective-permute-start
  857.4 8.3 collective-permute-start
  866.7 8.3 collective-permute-start
  876.0 8.3 collective-permute-start
  885.3 8.3 collective-permute-start
  894.6 8.3 collective-permute-start
  903.9 8.3 collective-permute-start
  913.2 8.3 collective-permute-start
  922.5 8.3 collective-permute-start
  931.8 8.3 collective-permute-start
  941.1 8.3 collective-permute-start
  950.4 8.3 collective-permute-start
  959.7 8.3 collective-permute-start
  969.0 8.3 collective-permute-start
  978.3 8.3 collective-permute-start
  987.6 8.3 collective-permute-start
  996.9 8.3 collective-permute-start
  1006.2 8.3 collective-permute-start
  1015.5 8.3 collective-permute-start
  1025.8 268.8 %all-gather.5.cloned.1.call-start = ((), (), s32[]{:S(2)}) async-start(), calls=%async_computation.1 | async-start | bytes 3993600 | tf_op jit(solution)/shard_map/all_gather | solution.py:108
  (84 other events, 835.0 us)
Sparse Core Ops, SparseCore 0:
  10.3 467.0 all-reduce.3
  1025.9 144.6 all-gather.2
  1173.0 121.5 all-gather.4
where the time goes:
time: 1310 us
  waiting for transfers between devices  796 us (61%)
  starting transfers between devices  478 us (36%)
  between operations  13.2 us (1%)
    ppermute x126, starting transfers between devices, shifted(): return lax.ppermute(block, axis, route)  477 us
    psum x1, waiting for transfers between devices, spread(): return lax.psum(kept, axis)  464 us
    all_gather x1, waiting for transfers between devices, local(): every_head = lax.all_gather(attended, 'mp', axis=1, tiled=True)  144 us
    all_gather x1, waiting for transfers between devices, local(): lax.all_gather(out_weight, 'ctx', axis=0, tiled=True)  124 us
    ppermute x126, waiting for transfers between devices, shifted(): return lax.ppermute(block, axis, route)  64.1 us
  transfers between devices with their start and end apart: 129, of which 66 were waited for; matrix products, arithmetic and copies ran while one was open for 0% of the time, Pallas kernels for 0%

commit v1 on v0

v1 whole, which is shorter than its diff:
```python
import functools

import jax
import jax.numpy as jnp
from jax import lax
from jax.experimental import pallas as pl
from jax.experimental.pallas import tpu as pltpu
from jax.sharding import Mesh
from jax.sharding import PartitionSpec as P

HD = 128
GROUP = 5
ROWS = 256
UNIT = 128
HALF = 64
MASKED = -1e30
SCALE = HD**-0.5 * 1.4426950408889634
STATE = HD + 16
VMEM = 48 * 1024 * 1024

FULL = ((0, UNIT, 0), (256, UNIT, 1), (512, UNIT, 2), (768, UNIT, 3), (1024, HALF, 4))
FRONT = ((0, UNIT, 0), (256, UNIT, 1))
BACK = ((0, UNIT, 2), (256, UNIT, 3), (512, HALF, 4))


def vmem():
    return pl.BlockSpec(memory_space=pltpu.VMEM)


def smem():
    return pl.BlockSpec(memory_space=pltpu.SMEM)


def params():
    return pltpu.CompilerParams(vmem_limit_bytes=VMEM)


def pick_kernel(core_ref, kept_ref, keys_ref, vals_ref, other_ref, out_ref):
    rows = lax.broadcasted_iota(jnp.int32, (ROWS, UNIT), 0)
    chosen = jnp.where(rows == kept_ref[...], 1.0, 0.0)
    chosen = jnp.transpose(chosen, (1, 0)).astype(jnp.bfloat16)
    dot = functools.partial(jnp.dot, preferred_element_type=jnp.float32)
    out_ref[0:UNIT, :] = dot(chosen, keys_ref[...]).astype(jnp.bfloat16)
    out_ref[UNIT : 2 * UNIT, :] = dot(chosen, vals_ref[...]).astype(jnp.bfloat16)

    @pl.when(core_ref[0] == 0)
    def _():
        out_ref[256 : 256 + HALF, :] = keys_ref[0:HALF, :]
        out_ref[256 + HALF : 384, :] = vals_ref[0:HALF, :]

    @pl.when(core_ref[0] != 0)
    def _():
        out_ref[256:384, :] = other_ref[...]


def pick(core, kept, keys, vals, other):
    return pl.pallas_call(
        pick_kernel,
        out_shape=jax.ShapeDtypeStruct((384, HD), jnp.bfloat16),
        in_specs=[smem(), vmem(), vmem(), vmem(), vmem()],
        out_specs=vmem(),
        compiler_params=params(),
        name="pick",
    )(core, kept, keys, vals, other)


def attend_kernel(*refs, layouts, sides, first, diag):
    refs = list(refs)
    flags = refs.pop(0)
    queries = [refs.pop(0) for _ in sides]
    own = (refs.pop(0), refs.pop(0)) if diag else None
    bundles = [refs.pop(0) for _ in layouts]
    states = None if first else [refs.pop(0) for _ in sides]
    outs = [refs.pop(0) for _ in sides]
    kcat, vcat, vt = refs
    parts = []
    at = 0
    for size in (UNIT, HALF):
        for which, layout in enumerate(layouts):
            for row, count, flag in layout:
                if count != size:
                    continue
                kcat[at : at + count, :] = bundles[which][row : row + count, :]
                vcat[at : at + count, :] = bundles[which][row + count : row + 2 * count, :]
                parts.append((at, count, which, flag))
                at += count
    if at % UNIT:
        kcat[at : at + HALF, :] = jnp.zeros((HALF, HD), jnp.bfloat16)
        vcat[at : at + HALF, :] = jnp.zeros((HALF, HD), jnp.bfloat16)
        parts.append((at, HALF, None, None))
        at += HALF
    shared = at
    if diag:
        kcat[at : at + ROWS, :] = own[0][...]
        vcat[at : at + ROWS, :] = own[1][...]
        at += ROWS
    vt[0:HD, :] = jnp.transpose(vcat[...].astype(jnp.float32), (1, 0)).astype(jnp.bfloat16)
    vt[HD:STATE, :] = jnp.ones((STATE - HD, at), jnp.bfloat16)

    tiles = [(n, side, head) for n, side in enumerate(sides) for head in range(GROUP)]

    def scores(tile):
        n, side, head = tile
        count = at if side == 0 else shared
        query = queries[n][:, head * HD : (head + 1) * HD]
        return lax.dot_general(
            kcat[0:count, :], query, (((1,), (1,)), ((), ())), preferred_element_type=jnp.float32
        )

    def finish(tile, raw):
        n, side, head = tile
        count = at if side == 0 else shared
        pieces = []
        for start, size, which, flag in parts:
            piece = raw[start : start + size, :]
            if which is None:
                pieces.append(jnp.full_like(piece, MASKED))
            else:
                usable = flags[(which * 2 + side) * 5 + flag]
                pieces.append(jnp.where(usable > 0, piece, MASKED))
        if diag and side == 0:
            key_at = lax.broadcasted_iota(jnp.int32, (ROWS, ROWS), 0)
            row_at = lax.broadcasted_iota(jnp.int32, (ROWS, ROWS), 1)
            pieces.append(jnp.where(key_at <= row_at, raw[shared:at, :], MASKED))
        top = functools.reduce(
            jnp.maximum, [jnp.max(piece, axis=0, keepdims=True) for piece in pieces]
        )
        if not first:
            old_top = states[n][head, HD + 8 : HD + 9, :]
            top = jnp.maximum(top, old_top)
        weights = jnp.concatenate(
            [jnp.exp2((piece - top) * SCALE).astype(jnp.bfloat16) for piece in pieces], 0
        )
        total = jnp.dot(vt[:, 0:count], weights, preferred_element_type=jnp.float32)
        if not first:
            total = total + states[n][head] * jnp.exp2((old_top - top) * SCALE)
        outs[n][head, 0 : HD + 8, :] = total[0 : HD + 8, :]
        outs[n][head, HD + 8 : STATE, :] = jnp.broadcast_to(top, (8, ROWS))

    raw = scores(tiles[0])
    for i, tile in enumerate(tiles):
        following = scores(tiles[i + 1]) if i + 1 < len(tiles) else None
        finish(tile, raw)
        raw = following


def attend(flags, queries, bundles, layouts, states=None, own=None, sides=(0, 1), name="attend"):
    first = states is None
    diag = own is not None
    keys = sum(count for layout in layouts for _, count, _ in layout)
    keys = -(-keys // UNIT) * UNIT + (ROWS if diag else 0)
    inputs = [flags, *queries, *(own or ()), *bundles, *(states or ())]
    state = jax.ShapeDtypeStruct((GROUP, STATE, ROWS), jnp.float32)
    tiles = len(sides) * GROUP
    return pl.pallas_call(
        functools.partial(attend_kernel, layouts=layouts, sides=sides, first=first, diag=diag),
        out_shape=[state] * len(sides),
        in_specs=[smem()] + [vmem()] * (len(inputs) - 1),
        out_specs=[vmem()] * len(sides),
        scratch_shapes=[
            pltpu.VMEM((keys, HD), jnp.bfloat16),
            pltpu.VMEM((keys, HD), jnp.bfloat16),
            pltpu.VMEM((STATE, keys), jnp.bfloat16),
        ],
        compiler_params=params(),
        cost_estimate=pl.CostEstimate(
            flops=8 * tiles * ROWS * keys * HD,
            bytes_accessed=4 * 1024 * 1024,
            transcendentals=tiles * ROWS * keys,
        ),
        name=name,
    )(*inputs)


def merge_kernel(mine_ref, theirs_ref, out_ref):
    for head in range(GROUP):
        top_a = mine_ref[head, HD + 8 : HD + 9, :]
        top_b = theirs_ref[head, HD + 8 : HD + 9, :]
        top = jnp.maximum(top_a, top_b)
        a = jnp.exp2((top_a - top) * SCALE)
        b = jnp.exp2((top_b - top) * SCALE)
        total = mine_ref[head, HD : HD + 1, :] * a + theirs_ref[head, HD : HD + 1, :] * b
        summed = mine_ref[head, 0:HD, :] * a + theirs_ref[head, 0:HD, :] * b
        attended = jnp.transpose(summed / total, (1, 0))
        out_ref[:, head * HD : (head + 1) * HD] = attended.astype(jnp.bfloat16)


def merge(mine, theirs):
    return pl.pallas_call(
        merge_kernel,
        out_shape=jax.ShapeDtypeStruct((ROWS, GROUP * HD), jnp.bfloat16),
        in_specs=[vmem(), vmem()],
        out_specs=vmem(),
        compiler_params=params(),
        name="merge",
    )(mine, theirs)


def project_kernel(at_ref, a0, a1, a2, a3, near_ref, far_ref, near_out, far_out, far_sum):
    step = pl.program_id(0)
    for i, a_ref in enumerate((a0, a1, a2, a3)):

        @pl.when(step == i)
        def _(i=i, a_ref=a_ref):
            near = jnp.dot(a_ref[...], near_ref[0, 0], preferred_element_type=jnp.float32)
            far = jnp.dot(a_ref[...], far_ref[0, 0], preferred_element_type=jnp.float32)
            if i == 0:
                near_out[...] = near
                far_sum[...] = far
            else:
                near_out[...] += near
                far_sum[...] += far
            if i == 3:
                far_out[...] = far_sum[...].astype(jnp.bfloat16)


def project(places, heads, weight):
    depth, width = weight.shape[2:]
    whole = pl.BlockSpec((ROWS, depth), lambda k, at: (0, 0))
    result = pl.BlockSpec((ROWS, width), lambda k, at: (0, 0))
    return pl.pallas_call(
        project_kernel,
        out_shape=[
            jax.ShapeDtypeStruct((ROWS, width), jnp.float32),
            jax.ShapeDtypeStruct((ROWS, width), jnp.bfloat16),
        ],
        grid_spec=pltpu.PrefetchScalarGridSpec(
            num_scalar_prefetch=1,
            grid=(4,),
            in_specs=[
                whole,
                whole,
                whole,
                whole,
                pl.BlockSpec((1, 1, depth, width), lambda k, at: (at[k], at[4], 0, 0)),
                pl.BlockSpec((1, 1, depth, width), lambda k, at: (3 - at[k], 1 - at[4], 0, 0)),
            ],
            out_specs=[result, result],
            scratch_shapes=[pltpu.VMEM((ROWS, width), jnp.float32)],
        ),
        compiler_params=params(),
        name="project",
    )(places, *heads, weight, weight)


def ring(size, distance):
    return [(i, (i + distance) % size) for i in range(size)]


def local(queries, keys, values, kept_rows, out_weight):
    y, z, c, x, h = (lax.axis_index(name) for name in ("y", "z", "c", "x", "h"))
    block = (y * 8 + z) * 2 + c
    swap = ring(2, 1)

    anchor = jnp.concatenate([keys[HALF : 2 * HALF], values[HALF : 2 * HALF]], 0)
    anchor = lax.ppermute(anchor, ("y", "z", "c"), [(0, 1)])
    unit = pick(c.reshape(1), kept_rows.reshape(1, UNIT), keys, values, anchor)

    came = [
        lax.ppermute(unit, "y", [(i, i + d) for i in range(4 - d)]) for d in (1, 2, 3)
    ]
    other_queries = lax.ppermute(queries, "c", swap)

    pairs = []
    for yy in range(4):
        for zz in range(8):
            hh = 0 if zz >= 4 else 1
            pairs.append(((yy * 8 + zz) * 2 + hh, ((3 - yy) * 8 + (zz ^ 4)) * 2 + 1 - hh))
    crossed = lax.ppermute(out_weight, ("y", "z", "h"), pairs)
    stays = (z >= 4) == (h == 1)
    weight = lax.all_gather(
        jnp.where(stays, out_weight, crossed), ("y", "z", "c"), axis=0, tiled=True
    ).reshape(4, 2, 640, out_weight.shape[1])

    first = functools.reduce(
        lambda held, d: jnp.where(y == d, came[d - 1][256:384], held), (1, 2, 3), unit[256:384]
    )
    bundle = jnp.concatenate([unit[:256]] + [part[:256] for part in came] + [first], 0)

    def flags_of(source):
        one = jnp.stack([source < z, y >= 1, y >= 2, y >= 3, source == 0])
        return jnp.concatenate([one, one])

    here = jnp.stack(
        [
            y < 0, y >= 1, y >= 2, y >= 3, (z == 0) & (block != 0),
            c == 0, y >= 1, y >= 2, y >= 3, (z == 0) & (block + 1 - 2 * c != 0),
        ]
    ).astype(jnp.int32)

    def flags_at(step):
        return jnp.concatenate(
            [flags_of((z + 8 - step) % 8), flags_of((z + step) % 8)]
        ).astype(jnp.int32)

    both = (queries, other_queries)
    right = lax.ppermute(bundle, "z", ring(8, 1))
    left = lax.ppermute(bundle, "z", ring(8, 7))
    states = attend(here, both, [bundle], (FULL,), own=(keys, values), name="attend0")
    for step in (1, 2):
        next_right = lax.ppermute(right, "z", ring(8, 1))
        next_left = lax.ppermute(left, "z", ring(8, 7))
        states = attend(
            flags_at(step), both, [right, left], (FULL, FULL), states, name=f"attend{step}"
        )
        right, left = next_right, next_left
    front = lax.ppermute(right[:512], "z", ring(8, 1))
    back = lax.ppermute(left[512:], "z", ring(8, 7))
    states = attend(flags_at(3), both, [right, left], (FULL, FULL), states, name="attend3")
    last = ([front, back], (FRONT, BACK))
    (theirs,) = attend(
        flags_at(4), (other_queries,), *last, (states[1],), sides=(1,), name="attend4b"
    )
    theirs = lax.ppermute(theirs, "c", swap)
    (mine,) = attend(flags_at(4), (queries,), *last, (states[0],), sides=(0,), name="attend4a")
    attended = merge(mine, theirs)

    heads = [attended] + [lax.ppermute(attended, "x", ring(4, d)) for d in (1, 3, 2)]
    places = jnp.stack([x, (x + 3) % 4, (x + 1) % 4, (x + 2) % 4, h]).astype(jnp.int32)
    near, far = project(places, heads, weight)
    return (near + lax.ppermute(far, "h", swap)).astype(jnp.bfloat16)


def solution(mesh):
    fine = Mesh(mesh.devices.reshape(4, 8, 2, 4, 2), ("y", "z", "c", "x", "h"))
    ctx, mp = ("y", "z", "c"), ("x", "h")
    placed = (P(ctx, mp), P(ctx, mp), P(ctx, mp), P(ctx, mp, None), P(ctx, mp))
    return jax.shard_map(
        local, mesh=fine, in_specs=placed, out_specs=P(ctx, mp), check_vma=False
    )
```

time: 1310 us -> 175 us (0.13)
  the two profiles are of different devices: /device:TPU:1 before, /device:TPU:40 now
where the time goes in v1:
time: 175 us; the launch traced here: 174 us
  starting transfers between devices  63 us (36%)
  waiting for transfers between devices  60.6 us (35%)
  Pallas kernels  25.5 us (15%)
  between operations  13.9 us (8%)
  local copies, waits for them, and re-layouts  9.29 us (5%)
    all_gather x1, waiting for transfers between devices, local(): lax.all_gather(jnp.where(stays, out_weight, crossed), ('y', 'z', 'c'), ax...  28 us
    pallas_call x6, Pallas kernels, attend(): pl.pallas_call(functools.partial(attend_kernel, layouts=layouts, sides=si...  22.2 us
    ppermute x1, waiting for transfers between devices, local(): return (near + lax.ppermute(far, 'h', swap)).astype(jnp.bfloat16)  14.9 us
    ppermute x1, starting transfers between devices, local(): crossed = lax.ppermute(out_weight, ('y', 'z', 'h'), pairs)  11.5 us
    ppermute x3, starting transfers between devices, local(): lax.ppermute(attended, 'x', ring(4, d))  10.7 us
    ppermute x3, waiting for transfers between devices, local(): lax.ppermute(attended, 'x', ring(4, d))  10.3 us
    ppermute x2, starting transfers between devices, local(): next_right = lax.ppermute(right, 'z', ring(8, 1))  7.77 us
    unnamed x20, local copies, waits for them, and re-layouts  7.14 us
  transfers between devices with their start and end apart: 20, of which 8 were waited for; matrix products, arithmetic and copies ran while one was open for 1% of the time, Pallas kernels for 13%

profile of v1, /device:TPU:40, one launch (start us, length us, event | category | flops | bytes accessed | tf_op | source)
XLA Modules:
  0.0 173.9 jit_solution(9363169709205713570)
XLA Ops:
  6.5 11.5 %collective-permute-start.17 = (bf16[80,384]{1,0:T(8,128)(2,1)}, bf16[80,384]{1,0:T(8,128)(2,1)S(1)}, u32[]{:S(2)}, u32[]{:S(2)}) collective-permute-start(bf16[80,384]{1,0:T(8,128)(2,1)} %param.9), channel_id=1, source_target_pairs={{1,448},{17,464},{33,480},{49,496},{64,385},{80,401},{96,417},{112... | collective-permute-start | bytes 184328 | tf_op jit(solution)/shard_map/ppermute | solution.py:269
  18.0 2.6 %collective-permute-done.17 = bf16[80,384]{1,0:T(8,128)(2,1)S(1)} collective-permute-done((bf16[80,384]{1,0:T(8,128)(2,1)}, bf16[80,384]{1,0:T(8,128)(2,1)S(1)}, u32[]{:S(2)}, u32[]{:S(2)}) %collective-permute-start.17) | collective-permute-done | bytes 61472 | tf_op jit(solution)/shard_map/ppermute | solution.py:269
  20.7 0.6 broadcast_select_fusion
  21.3 0.7 slice.36
  22.1 0.7 slice.37
  22.8 0.7 collective-permute-start
  23.5 0.8 copy-done.1
  24.3 0.8 copy-done.3
  25.1 0.7 copy-done.5
  25.8 0.2 pick.1
  26.0 2.6 %collective-permute-start.1 = (bf16[384,128]{1,0:T(8,128)(2,1)S(1)}, bf16[384,128]{1,0:T(8,128)(2,1)S(1)}, u32[]{:S(2)}, u32[]{:S(2)}) collective-permute-start(bf16[384,128]{1,0:T(8,128)(2,1)S(1)} %pick.1), channel_id=1, source_target_pairs={{0,128},{128,256},{256,384},{1,129},{129,257},{257,385},{2,130},{1... | collective-permute-start | bytes 294920 | tf_op jit(solution)/shard_map/ppermute | solution.py:260
  28.7 1.3 collective-permute-start.2
  30.0 0.7 collective-permute-start.3
  30.6 3.6 %collective-permute-done.1 = bf16[384,128]{1,0:T(8,128)(2,1)S(1)} collective-permute-done((bf16[384,128]{1,0:T(8,128)(2,1)S(1)}, bf16[384,128]{1,0:T(8,128)(2,1)S(1)}, u32[]{:S(2)}, u32[]{:S(2)}) %collective-permute-start.1) | collective-permute-done | bytes 98336 | tf_op jit(solution)/shard_map/ppermute | solution.py:260
  34.4 1.9 %collective-permute-start.8 = (bf16[1152,128]{1,0:T(8,128)(2,1)S(1)}, bf16[1152,128]{1,0:T(8,128)(2,1)S(1)}, u32[]{:S(2)}, u32[]{:S(2)}) collective-permute-start(bf16[1152,128]{1,0:T(8,128)(2,1)S(1)} %fusion.2.refs_5_), channel_id=1, source_target_pairs={{0,112},{16,0},{32,16},{48,32},{64,48},{80,64},{96,80},{112,96},{1... | collective-permute-start | bytes 884744 | tf_op jit(solution)/shard_map/ppermute | solution.py:298
  36.3 6.2 %collective-permute-start.4 = (bf16[1152,128]{1,0:T(8,128)(2,1)S(1)}, bf16[1152,128]{1,0:T(8,128)(2,1)S(1)}, u32[]{:S(2)}, u32[]{:S(2)}) collective-permute-start(bf16[1152,128]{1,0:T(8,128)(2,1)S(1)} %fusion.2.refs_5_), channel_id=1, source_target_pairs={{0,16},{16,32},{32,48},{48,64},{64,80},{80,96},{96,112},{112,0},{1... | collective-permute-start | bytes 884744 | tf_op jit(solution)/shard_map/ppermute | solution.py:297
  42.5 1.9 %collective-permute-start.12 = (bf16[256,640]{1,0:T(8,128)(2,1)}, bf16[256,640]{1,0:T(8,128)(2,1)S(1)}, u32[]{:S(2)}, u32[]{:S(2)}) collective-permute-start(bf16[256,640]{1,0:T(8,128)(2,1)} %refs_1_.9), channel_id=1, source_target_pairs={{0,8},{8,0},{1,9},{9,1},{2,10},{10,2},{3,11},{11,3},{4,12},{12,4},... | collective-permute-start | bytes 983048 | tf_op jit(solution)/shard_map/ppermute | solution.py:262
  44.5 0.8 collective-permute-done.8.refs_4_
  45.3 2.7 %collective-permute-start.9 = (bf16[1152,128]{1,0:T(8,128)(2,1)S(1)}, bf16[1152,128]{1,0:T(8,128)(2,1)S(1)}, u32[]{:S(2)}, u32[]{:S(2)}) collective-permute-start(bf16[1152,128]{1,0:T(8,128)(2,1)S(1)} %collective-permute-done.8.refs_4_), channel_id=1, source_target_pairs={{0,112},{16,0},{32,16},{48,32},{64,48},{80,64},{96,80},{112,96},{1... | collective-permute-start | bytes 884744 | tf_op jit(solution)/shard_map/ppermute | solution.py:302
  48.0 4.3 %collective-permute-start.5 = (bf16[1152,128]{1,0:T(8,128)(2,1)S(1)}, bf16[1152,128]{1,0:T(8,128)(2,1)S(1)}, u32[]{:S(2)}, u32[]{:S(2)}) collective-permute-start(bf16[1152,128]{1,0:T(8,128)(2,1)S(1)} %collective-permute-done.4.refs_3_), channel_id=1, source_target_pairs={{0,16},{16,32},{32,48},{48,64},{64,80},{80,96},{96,112},{112,0},{1... | collective-permute-start | bytes 884744 | tf_op jit(solution)/shard_map/ppermute | solution.py:301
  52.7 0.1 concatenate.28
  53.1 0.8 copy-done.2
  54.0 0.8 copy-done.4
  54.8 1.0 copy-done.6
  55.8 3.5 %attend0.1 = (f32[5,144,256]{2,1,0:T(8,128)S(1)}, f32[5,144,256]{2,1,0:T(8,128)S(1)}) custom-call(s32[10]{0:T(128)S(1)} %convert_element_type.26.refs_0_, bf16[256,640]{1,0:T(8,128)(2,1)S(1)} %copy-done.6, bf16[256,640]{1,0:T(8,128)(2,1)S(1)} %collective-permute-done.12.refs_2_.refs_1_, bf16[256,128]{1,0:T(8,128)(2,1)S(1)} %copy-done.2, ...), custom_call_target="tpu_custom_call" | custom-call | flops 2348810240 | bytes 4194304 | tf_op jit(solution)/shard_map/attend0/pallas_call | solution.py:155
  59.3 2.7 %collective-permute-start.10 = (bf16[1152,128]{1,0:T(8,128)(2,1)S(1)}, bf16[1152,128]{1,0:T(8,128)(2,1)S(1)}, u32[]{:S(2)}, u32[]{:S(2)}) collective-permute-start(bf16[1152,128]{1,0:T(8,128)(2,1)S(1)} %collective-permute-done.9.refs_4_), channel_id=1, source_target_pairs={{0,112},{16,0},{32,16},{48,32},{64,48},{80,64},{96,80},{112,96},{1... | collective-permute-start | bytes 884744 | tf_op jit(solution)/shard_map/ppermute | solution.py:302
  62.1 3.4 %collective-permute-start.6 = (bf16[1152,128]{1,0:T(8,128)(2,1)S(1)}, bf16[1152,128]{1,0:T(8,128)(2,1)S(1)}, u32[]{:S(2)}, u32[]{:S(2)}) collective-permute-start(bf16[1152,128]{1,0:T(8,128)(2,1)S(1)} %collective-permute-done.5.refs_3_), channel_id=1, source_target_pairs={{0,16},{16,32},{32,48},{48,64},{64,80},{80,96},{96,112},{112,0},{1... | collective-permute-start | bytes 884744 | tf_op jit(solution)/shard_map/ppermute | solution.py:301
  65.5 5.0 %attend1.1 = (f32[5,144,256]{2,1,0:T(8,128)S(1)}, f32[5,144,256]{2,1,0:T(8,128)S(1)}) custom-call(s32[20]{0:T(128)S(1)} %convert_element_type.25.refs_0_, bf16[256,640]{1,0:T(8,128)(2,1)S(1)} %copy-done.7, bf16[256,640]{1,0:T(8,128)(2,1)S(1)} %collective-permute-done.12.refs_2_.refs_1_, bf16[1152,128]{1,0:T(8,128)(2,1)S(1)} %collective-permute-done.4.refs_3_, ...), custom_call_target="tpu_custom_call" | custom-call | flops 3019898880 | bytes 4194304 | tf_op jit(solution)/shard_map/attend1/pallas_call | solution.py:155
  70.5 5.0 %attend2.1 = (f32[5,144,256]{2,1,0:T(8,128)S(1)}, f32[5,144,256]{2,1,0:T(8,128)S(1)}) custom-call(s32[20]{0:T(128)S(1)} %convert_element_type.24.refs_0_, bf16[256,640]{1,0:T(8,128)(2,1)S(1)} %copy-done.7, bf16[256,640]{1,0:T(8,128)(2,1)S(1)} %collective-permute-done.12.refs_2_.refs_1_, bf16[1152,128]{1,0:T(8,128)(2,1)S(1)} %collective-permute-done.5.refs_3_, ...), custom_call_target="tpu_custom_call" | custom-call | flops 3019898880 | bytes 4194304 | tf_op jit(solution)/shard_map/attend2/pallas_call | solution.py:155
  75.5 3.8 %collective-permute-start.11 = (bf16[640,128]{1,0:T(8,128)(2,1)S(1)}, bf16[640,128]{1,0:T(8,128)(2,1)S(1)}, u32[]{:S(2)}, u32[]{:S(2)}) collective-permute-start(bf16[640,128]{1,0:T(8,128)(2,1)S(1)} %slice.57), channel_id=1, source_target_pairs={{0,112},{16,0},{32,16},{48,32},{64,48},{80,64},{96,80},{112,96},{1... | collective-permute-start | bytes 491528 | tf_op jit(solution)/shard_map/ppermute | solution.py:308
  79.3 4.4 %collective-permute-start.7 = (bf16[512,128]{1,0:T(8,128)(2,1)S(1)}, bf16[512,128]{1,0:T(8,128)(2,1)S(1)}, u32[]{:S(2)}, u32[]{:S(2)}) collective-permute-start(bf16[512,128]{1,0:T(8,128)(2,1)S(1)} %slice.56), channel_id=1, source_target_pairs={{0,16},{16,32},{32,48},{48,64},{64,80},{80,96},{96,112},{112,0},{1... | collective-permute-start | bytes 393224 | tf_op jit(solution)/shard_map/ppermute | solution.py:307
  83.8 5.0 %attend3.1 = (f32[5,144,256]{2,1,0:T(8,128)S(1)}, f32[5,144,256]{2,1,0:T(8,128)S(1)}) custom-call(s32[20]{0:T(128)S(1)} %convert_element_type.23.refs_0_, bf16[256,640]{1,0:T(8,128)(2,1)S(1)} %copy-done.7, bf16[256,640]{1,0:T(8,128)(2,1)S(1)} %collective-permute-done.12.refs_2_.refs_1_, bf16[1152,128]{1,0:T(8,128)(2,1)S(1)} %collective-permute-done.6.refs_3_, ...), custom_call_target="tpu_custom_call" | custom-call | flops 3019898880 | bytes 4194304 | tf_op jit(solution)/shard_map/attend3/pallas_call | solution.py:155
  88.8 1.9 %attend4b.1 = f32[5,144,256]{2,1,0:T(8,128)S(1)} custom-call(s32[20]{0:T(128)S(1)} %convert_element_type.22.refs_0_, bf16[256,640]{1,0:T(8,128)(2,1)S(1)} %collective-permute-done.12.refs_2_.refs_1_, bf16[512,128]{1,0:T(8,128)(2,1)S(1)} %collective-permute-done.7.refs_2_, bf16[640,128]{1,0:T(8,128)(2,1)S(1)} %collective-permute-done.11.refs_3_, ...), custom_call_target="tpu_custom_call" | custom-call | flops 838860800 | bytes 4194304 | tf_op jit(solution)/shard_map/attend4b/pallas_call | solution.py:155
  90.7 1.9 %collective-permute-start.13 = (f32[5,144,256]{2,1,0:T(8,128)S(1)}, f32[5,144,256]{2,1,0:T(8,128)S(1)}, u32[]{:S(2)}, u32[]{:S(2)}) collective-permute-start(f32[5,144,256]{2,1,0:T(8,128)S(1)} %attend4b.1), channel_id=1, source_target_pairs={{0,8},{8,0},{1,9},{9,1},{2,10},{10,2},{3,11},{11,3},{4,12},{12,4},... | collective-permute-start | bytes 2211848 | tf_op jit(solution)/shard_map/ppermute | solution.py:314
  92.6 1.9 %attend4a.1.mine_ref = f32[5,144,256]{2,1,0:T(8,128)S(1)} custom-call(s32[20]{0:T(128)S(1)} %convert_element_type.22.refs_0_, bf16[256,640]{1,0:T(8,128)(2,1)S(1)} %copy-done.7, bf16[512,128]{1,0:T(8,128)(2,1)S(1)} %collective-permute-done.7.refs_2_, bf16[640,128]{1,0:T(8,128)(2,1)S(1)} %collective-permute-done.11.refs_3_, ...), custom_call_target="tpu_custom_call" | custom-call | flops 838860800 | bytes 4194304 | tf_op jit(solution)/shard_map/attend4a/pallas_call | solution.py:155
  94.5 0.3 collective-permute-done.13.theirs_ref
  94.8 0.2 merge.1.a0
  95.0 3.4 %collective-permute-start.14 = (bf16[256,640]{1,0:T(8,128)(2,1)S(1)}, bf16[256,640]{1,0:T(8,128)(2,1)S(1)}, u32[]{:S(2)}, u32[]{:S(2)}) collective-permute-start(bf16[256,640]{1,0:T(8,128)(2,1)S(1)} %merge.1.a0), channel_id=1, source_target_pairs={{0,2},{2,4},{4,6},{6,0},{1,3},{3,5},{5,7},{7,1},{8,10},{10,12},{12... | collective-permute-start | bytes 983048 | tf_op jit(solution)/shard_map/ppermute | solution.py:318
  98.4 3.7 %collective-permute-start.15 = (bf16[256,640]{1,0:T(8,128)(2,1)S(1)}, bf16[256,640]{1,0:T(8,128)(2,1)S(1)}, u32[]{:S(2)}, u32[]{:S(2)}) collective-permute-start(bf16[256,640]{1,0:T(8,128)(2,1)S(1)} %merge.1.a0), channel_id=1, source_target_pairs={{0,6},{2,0},{4,2},{6,4},{1,7},{3,1},{5,3},{7,5},{8,14},{10,8},{12,... | collective-permute-start | bytes 983048 | tf_op jit(solution)/shard_map/ppermute | solution.py:318
  102.1 3.7 %collective-permute-start.16 = (bf16[256,640]{1,0:T(8,128)(2,1)S(1)}, bf16[256,640]{1,0:T(8,128)(2,1)S(1)}, u32[]{:S(2)}, u32[]{:S(2)}) collective-permute-start(bf16[256,640]{1,0:T(8,128)(2,1)S(1)} %merge.1.a0), channel_id=1, source_target_pairs={{0,4},{2,6},{4,0},{6,2},{1,5},{3,7},{5,1},{7,3},{8,12},{10,14},{12... | collective-permute-start | bytes 983048 | tf_op jit(solution)/shard_map/ppermute | solution.py:318
  105.9 2.1 %collective-permute-done.14.a1 = bf16[256,640]{1,0:T(8,128)(2,1)S(1)} collective-permute-done((bf16[256,640]{1,0:T(8,128)(2,1)S(1)}, bf16[256,640]{1,0:T(8,128)(2,1)S(1)}, u32[]{:S(2)}, u32[]{:S(2)}) %collective-permute-start.14) | collective-permute-done | bytes 327712 | tf_op jit(solution)/shard_map/ppermute | solution.py:318
  108.0 8.2 %collective-permute-done.15.a2 = bf16[256,640]{1,0:T(8,128)(2,1)S(1)} collective-permute-done((bf16[256,640]{1,0:T(8,128)(2,1)S(1)}, bf16[256,640]{1,0:T(8,128)(2,1)S(1)}, u32[]{:S(2)}, u32[]{:S(2)}) %collective-permute-start.15) | collective-permute-done | bytes 327712 | tf_op jit(solution)/shard_map/ppermute | solution.py:318
  116.2 28.0 %all-gather.2.cloned.1.call-done = bf16[5120,384]{1,0:T(8,128)(2,1)} async-done(((bf16[80,384]{1,0:T(8,128)(2,1)}), bf16[5120,384]{1,0:T(8,128)(2,1)}) %all-gather.2.cloned.1.call-update) | async-done | bytes 3932176 | tf_op jit(solution)/shard_map/all_gather | solution.py:271
  144.3 2.1 %copy-done = bf16[5120,384]{1,0:T(8,128)(2,1)S(1)} copy-done((bf16[5120,384]{1,0:T(8,128)(2,1)S(1)}, bf16[5120,384]{1,0:T(8,128)(2,1)}, u32[]{:S(2)}) %copy-start) | copy-done | bytes 3932184
  146.4 2.8 %project.1 = (f32[256,384]{1,0:T(8,128)S(1)}, bf16[256,384]{1,0:T(8,128)(2,1)S(1)}) custom-call(s32[5]{0:T(128)S(1)} %stack.61.at_ref, bf16[256,640]{1,0:T(8,128)(2,1)S(1)} %merge.1.a0, bf16[256,640]{1,0:T(8,128)(2,1)S(1)} %collective-permute-done.14.a1, bf16[256,640]{1,0:T(8,128)(2,1)S(1)} %collective-permute-done.15.a2, ...), custom_call_target="tpu_custom_call" | custom-call | tf_op jit(solution)/shard_map/project/pallas_call | solution.py:221
  149.2 2.2 %collective-permute-start.18 = (bf16[256,384]{1,0:T(8,128)(2,1)S(1)}, bf16[256,384]{1,0:T(8,128)(2,1)S(1)}, u32[]{:S(2)}, u32[]{:S(2)}) collective-permute-start(bf16[256,384]{1,0:T(8,128)(2,1)S(1)} %get-tuple-element.24), channel_id=1, source_target_pairs={{0,1},{1,0},{2,3},{3,2},{4,5},{5,4},{6,7},{7,6},{8,9},{9,8},{10,11... | collective-permute-start | bytes 589832 | tf_op jit(solution)/shard_map/ppermute | solution.py:321
  151.4 14.9 %collective-permute-done.18 = bf16[256,384]{1,0:T(8,128)(2,1)S(1)} collective-permute-done((bf16[256,384]{1,0:T(8,128)(2,1)S(1)}, bf16[256,384]{1,0:T(8,128)(2,1)S(1)}, u32[]{:S(2)}, u32[]{:S(2)}) %collective-permute-start.18) | collective-permute-done | bytes 196640 | tf_op jit(solution)/shard_map/ppermute | solution.py:321
  166.3 0.7 add_convert_fusion
  (41 shorter events, 0.8 us)
Async XLA Ops:
  6.5 137.7 %all-gather.2.cloned.1.call-start = ((), (), s32[]{:S(2)}) async-start(), calls=%async_computation | async-start | bytes 3993600 | tf_op jit(solution)/shard_map/all_gather | solution.py:271
  6.5 14.1 %collective-permute-start.17 = (bf16[80,384]{1,0:T(8,128)(2,1)}, bf16[80,384]{1,0:T(8,128)(2,1)S(1)}, u32[]{:S(2)}, u32[]{:S(2)}) collective-permute-start(bf16[80,384]{1,0:T(8,128)(2,1)} %param.9), channel_id=1, source_target_pairs={{1,448},{17,464},{33,480},{49,496},{64,385},{80,401},{96,417},{112... | collective-permute-start | bytes 184328 | tf_op jit(solution)/shard_map/ppermute | solution.py:269
  22.8 0.7 collective-permute-start
  23.5 0.8 copy-start.1
  24.3 0.8 copy-start.3
  25.1 0.7 copy-start.5
  26.0 8.2 %collective-permute-start.1 = (bf16[384,128]{1,0:T(8,128)(2,1)S(1)}, bf16[384,128]{1,0:T(8,128)(2,1)S(1)}, u32[]{:S(2)}, u32[]{:S(2)}) collective-permute-start(bf16[384,128]{1,0:T(8,128)(2,1)S(1)} %pick.1), channel_id=1, source_target_pairs={{0,128},{128,256},{256,384},{1,129},{129,257},{257,385},{2,130},{1... | collective-permute-start | bytes 294920 | tf_op jit(solution)/shard_map/ppermute | solution.py:260
  28.7 5.6 %collective-permute-start.2 = (bf16[384,128]{1,0:T(8,128)(2,1)S(1)}, bf16[384,128]{1,0:T(8,128)(2,1)S(1)}, u32[]{:S(2)}, u32[]{:S(2)}) collective-permute-start(bf16[384,128]{1,0:T(8,128)(2,1)S(1)} %pick.1), channel_id=1, source_target_pairs={{0,256},{128,384},{1,257},{129,385},{2,258},{130,386},{3,259},{131... | collective-permute-start | bytes 294920 | tf_op jit(solution)/shard_map/ppermute | solution.py:260
  30.0 4.3 %collective-permute-start.3 = (bf16[384,128]{1,0:T(8,128)(2,1)S(1)}, bf16[384,128]{1,0:T(8,128)(2,1)S(1)}, u32[]{:S(2)}, u32[]{:S(2)}) collective-permute-start(bf16[384,128]{1,0:T(8,128)(2,1)S(1)} %pick.1), channel_id=1, source_target_pairs={{0,384},{1,385},{2,386},{3,387},{4,388},{5,389},{6,390},{7,391},{8... | collective-permute-start | bytes 294920 | tf_op jit(solution)/shard_map/ppermute | solution.py:260
  34.4 10.9 %collective-permute-start.8 = (bf16[1152,128]{1,0:T(8,128)(2,1)S(1)}, bf16[1152,128]{1,0:T(8,128)(2,1)S(1)}, u32[]{:S(2)}, u32[]{:S(2)}) collective-permute-start(bf16[1152,128]{1,0:T(8,128)(2,1)S(1)} %fusion.2.refs_5_), channel_id=1, source_target_pairs={{0,112},{16,0},{32,16},{48,32},{64,48},{80,64},{96,80},{112,96},{1... | collective-permute-start | bytes 884744 | tf_op jit(solution)/shard_map/ppermute | solution.py:298
  36.3 11.7 %collective-permute-start.4 = (bf16[1152,128]{1,0:T(8,128)(2,1)S(1)}, bf16[1152,128]{1,0:T(8,128)(2,1)S(1)}, u32[]{:S(2)}, u32[]{:S(2)}) collective-permute-start(bf16[1152,128]{1,0:T(8,128)(2,1)S(1)} %fusion.2.refs_5_), channel_id=1, source_target_pairs={{0,16},{16,32},{32,48},{48,64},{64,80},{80,96},{96,112},{112,0},{1... | collective-permute-start | bytes 884744 | tf_op jit(solution)/shard_map/ppermute | solution.py:297
  42.5 10.6 %collective-permute-start.12 = (bf16[256,640]{1,0:T(8,128)(2,1)}, bf16[256,640]{1,0:T(8,128)(2,1)S(1)}, u32[]{:S(2)}, u32[]{:S(2)}) collective-permute-start(bf16[256,640]{1,0:T(8,128)(2,1)} %refs_1_.9), channel_id=1, source_target_pairs={{0,8},{8,0},{1,9},{9,1},{2,10},{10,2},{3,11},{11,3},{4,12},{12,4},... | collective-permute-start | bytes 983048 | tf_op jit(solution)/shard_map/ppermute | solution.py:262
  45.3 14.0 %collective-permute-start.9 = (bf16[1152,128]{1,0:T(8,128)(2,1)S(1)}, bf16[1152,128]{1,0:T(8,128)(2,1)S(1)}, u32[]{:S(2)}, u32[]{:S(2)}) collective-permute-start(bf16[1152,128]{1,0:T(8,128)(2,1)S(1)} %collective-permute-done.8.refs_4_), channel_id=1, source_target_pairs={{0,112},{16,0},{32,16},{48,32},{64,48},{80,64},{96,80},{112,96},{1... | collective-permute-start | bytes 884744 | tf_op jit(solution)/shard_map/ppermute | solution.py:302
  48.0 14.0 %collective-permute-start.5 = (bf16[1152,128]{1,0:T(8,128)(2,1)S(1)}, bf16[1152,128]{1,0:T(8,128)(2,1)S(1)}, u32[]{:S(2)}, u32[]{:S(2)}) collective-permute-start(bf16[1152,128]{1,0:T(8,128)(2,1)S(1)} %collective-permute-done.4.refs_3_), channel_id=1, source_target_pairs={{0,16},{16,32},{32,48},{48,64},{64,80},{80,96},{96,112},{112,0},{1... | collective-permute-start | bytes 884744 | tf_op jit(solution)/shard_map/ppermute | solution.py:301
  53.1 0.8 copy-start.2
  54.0 0.8 copy-start.4
  54.8 1.0 copy-start.6
  55.8 9.7 %copy-start.7 = (bf16[256,640]{1,0:T(8,128)(2,1)S(1)}, bf16[256,640]{1,0:T(8,128)(2,1)}, u32[]{:S(2)}) copy-start(bf16[256,640]{1,0:T(8,128)(2,1)} %refs_1_.9) | copy-start | bytes 983044
  59.3 16.1 %collective-permute-start.10 = (bf16[1152,128]{1,0:T(8,128)(2,1)S(1)}, bf16[1152,128]{1,0:T(8,128)(2,1)S(1)}, u32[]{:S(2)}, u32[]{:S(2)}) collective-permute-start(bf16[1152,128]{1,0:T(8,128)(2,1)S(1)} %collective-permute-done.9.refs_4_), channel_id=1, source_target_pairs={{0,112},{16,0},{32,16},{48,32},{64,48},{80,64},{96,80},{112,96},{1... | collective-permute-start | bytes 884744 | tf_op jit(solution)/shard_map/ppermute | solution.py:302
  62.1 17.2 %collective-permute-start.6 = (bf16[1152,128]{1,0:T(8,128)(2,1)S(1)}, bf16[1152,128]{1,0:T(8,128)(2,1)S(1)}, u32[]{:S(2)}, u32[]{:S(2)}) collective-permute-start(bf16[1152,128]{1,0:T(8,128)(2,1)S(1)} %collective-permute-done.5.refs_3_), channel_id=1, source_target_pairs={{0,16},{16,32},{32,48},{48,64},{64,80},{80,96},{96,112},{112,0},{1... | collective-permute-start | bytes 884744 | tf_op jit(solution)/shard_map/ppermute | solution.py:301
  75.5 13.3 %collective-permute-start.11 = (bf16[640,128]{1,0:T(8,128)(2,1)S(1)}, bf16[640,128]{1,0:T(8,128)(2,1)S(1)}, u32[]{:S(2)}, u32[]{:S(2)}) collective-permute-start(bf16[640,128]{1,0:T(8,128)(2,1)S(1)} %slice.57), channel_id=1, source_target_pairs={{0,112},{16,0},{32,16},{48,32},{64,48},{80,64},{96,80},{112,96},{1... | collective-permute-start | bytes 491528 | tf_op jit(solution)/shard_map/ppermute | solution.py:308
  79.3 9.4 %collective-permute-start.7 = (bf16[512,128]{1,0:T(8,128)(2,1)S(1)}, bf16[512,128]{1,0:T(8,128)(2,1)S(1)}, u32[]{:S(2)}, u32[]{:S(2)}) collective-permute-start(bf16[512,128]{1,0:T(8,128)(2,1)S(1)} %slice.56), channel_id=1, source_target_pairs={{0,16},{16,32},{32,48},{48,64},{64,80},{80,96},{96,112},{112,0},{1... | collective-permute-start | bytes 393224 | tf_op jit(solution)/shard_map/ppermute | solution.py:307
  90.7 4.1 %collective-permute-start.13 = (f32[5,144,256]{2,1,0:T(8,128)S(1)}, f32[5,144,256]{2,1,0:T(8,128)S(1)}, u32[]{:S(2)}, u32[]{:S(2)}) collective-permute-start(f32[5,144,256]{2,1,0:T(8,128)S(1)} %attend4b.1), channel_id=1, source_target_pairs={{0,8},{8,0},{1,9},{9,1},{2,10},{10,2},{3,11},{11,3},{4,12},{12,4},... | collective-permute-start | bytes 2211848 | tf_op jit(solution)/shard_map/ppermute | solution.py:314
  95.0 13.0 %collective-permute-start.14 = (bf16[256,640]{1,0:T(8,128)(2,1)S(1)}, bf16[256,640]{1,0:T(8,128)(2,1)S(1)}, u32[]{:S(2)}, u32[]{:S(2)}) collective-permute-start(bf16[256,640]{1,0:T(8,128)(2,1)S(1)} %merge.1.a0), channel_id=1, source_target_pairs={{0,2},{2,4},{4,6},{6,0},{1,3},{3,5},{5,7},{7,1},{8,10},{10,12},{12... | collective-permute-start | bytes 983048 | tf_op jit(solution)/shard_map/ppermute | solution.py:318
  98.4 17.8 %collective-permute-start.15 = (bf16[256,640]{1,0:T(8,128)(2,1)S(1)}, bf16[256,640]{1,0:T(8,128)(2,1)S(1)}, u32[]{:S(2)}, u32[]{:S(2)}) collective-permute-start(bf16[256,640]{1,0:T(8,128)(2,1)S(1)} %merge.1.a0), channel_id=1, source_target_pairs={{0,6},{2,0},{4,2},{6,4},{1,7},{3,1},{5,3},{7,5},{8,14},{10,8},{12,... | collective-permute-start | bytes 983048 | tf_op jit(solution)/shard_map/ppermute | solution.py:318
  102.1 14.2 %collective-permute-start.16 = (bf16[256,640]{1,0:T(8,128)(2,1)S(1)}, bf16[256,640]{1,0:T(8,128)(2,1)S(1)}, u32[]{:S(2)}, u32[]{:S(2)}) collective-permute-start(bf16[256,640]{1,0:T(8,128)(2,1)S(1)} %merge.1.a0), channel_id=1, source_target_pairs={{0,4},{2,6},{4,0},{6,2},{1,5},{3,7},{5,1},{7,3},{8,12},{10,14},{12... | collective-permute-start | bytes 983048 | tf_op jit(solution)/shard_map/ppermute | solution.py:318
  144.3 2.1 %copy-start = (bf16[5120,384]{1,0:T(8,128)(2,1)S(1)}, bf16[5120,384]{1,0:T(8,128)(2,1)}, u32[]{:S(2)}) copy-start(bf16[5120,384]{1,0:T(8,128)(2,1)} %all-gather.2.cloned.1.call-done) | copy-start | bytes 11796484
  149.2 17.1 %collective-permute-start.18 = (bf16[256,384]{1,0:T(8,128)(2,1)S(1)}, bf16[256,384]{1,0:T(8,128)(2,1)S(1)}, u32[]{:S(2)}, u32[]{:S(2)}) collective-permute-start(bf16[256,384]{1,0:T(8,128)(2,1)S(1)} %get-tuple-element.24), channel_id=1, source_target_pairs={{0,1},{1,0},{2,3},{3,2},{4,5},{5,4},{6,7},{7,6},{8,9},{9,8},{10,11... | collective-permute-start | bytes 589832 | tf_op jit(solution)/shard_map/ppermute | solution.py:321
Sparse Core Ops, SparseCore 0:
  21.5 122.7 all-gather.1

commit v2 on v1

--- a/solution.py
+++ b/solution.py
@@ -16,7 +16,8 @@
 MASKED = -1e30
 SCALE = HD**-0.5 * 1.4426950408889634
 STATE = HD + 16
-VMEM = 48 * 1024 * 1024
+WEIGHT_STEP = 1
+VMEM = 20 * 1024 * 1024
 
 FULL = ((0, UNIT, 0), (256, UNIT, 1), (512, UNIT, 2), (768, UNIT, 3), (1024, HALF, 4))
 FRONT = ((0, UNIT, 0), (256, UNIT, 1))
@@ -35,10 +36,29 @@
     return pltpu.CompilerParams(vmem_limit_bytes=VMEM)
 
 
-def pick_kernel(core_ref, kept_ref, keys_ref, vals_ref, other_ref, out_ref):
+def hbm():
+    return pl.BlockSpec(memory_space=pltpu.HBM)
+
+
+def load(pairs, sems):
+    copies = [pltpu.make_async_copy(src, dst, sems.at[i]) for i, (src, dst) in enumerate(pairs)]
+    for copy in copies:
+        copy.start()
+    return copies
+
+
+def pick_kernel(core_ref, kept_ref, keys_hbm, vals_hbm, far_keys, far_vals, weight_ref, out_ref, *scratch):
+    keys_ref, vals_ref, sems = scratch
+    copies = load(((keys_hbm, keys_ref), (vals_hbm, vals_ref)), sems)
     rows = lax.broadcasted_iota(jnp.int32, (ROWS, UNIT), 0)
     chosen = jnp.where(rows == kept_ref[...], 1.0, 0.0)
     chosen = jnp.transpose(chosen, (1, 0)).astype(jnp.bfloat16)
+    shard = weight_ref.shape[0]
+    for i in range(3):
+        at = 384 + i * shard
+        out_ref[at : at + shard, :] = weight_ref[:, i * HD : (i + 1) * HD]
+    for copy in copies:
+        copy.wait()
     dot = functools.partial(jnp.dot, preferred_element_type=jnp.float32)
     out_ref[0:UNIT, :] = dot(chosen, keys_ref[...]).astype(jnp.bfloat16)
     out_ref[UNIT : 2 * UNIT, :] = dot(chosen, vals_ref[...]).astype(jnp.bfloat16)
@@ -50,18 +70,24 @@
 
     @pl.when(core_ref[0] != 0)
     def _():
-        out_ref[256:384, :] = other_ref[...]
-
-
-def pick(core, kept, keys, vals, other):
+        out_ref[256 : 256 + HALF, :] = far_keys[HALF : 2 * HALF, :]
+        out_ref[256 + HALF : 384, :] = far_vals[HALF : 2 * HALF, :]
+
+
+def pick(core, kept, keys, vals, far_keys, far_vals, weight):
     return pl.pallas_call(
         pick_kernel,
-        out_shape=jax.ShapeDtypeStruct((384, HD), jnp.bfloat16),
-        in_specs=[smem(), vmem(), vmem(), vmem(), vmem()],
+        out_shape=jax.ShapeDtypeStruct((384 + 3 * weight.shape[0], HD), jnp.bfloat16),
+        in_specs=[smem(), vmem(), hbm(), hbm(), vmem(), vmem(), vmem()],
         out_specs=vmem(),
+        scratch_shapes=[
+            pltpu.VMEM((ROWS, HD), jnp.bfloat16),
+            pltpu.VMEM((ROWS, HD), jnp.bfloat16),
+            pltpu.SemaphoreType.DMA((2,)),
+        ],
         compiler_params=params(),
         name="pick",
-    )(core, kept, keys, vals, other)
+    )(core, kept, keys, vals, far_keys, far_vals, weight)
 
 
 def attend_kernel(*refs, layouts, sides, first, diag):
@@ -72,7 +98,9 @@
     bundles = [refs.pop(0) for _ in layouts]
     states = None if first else [refs.pop(0) for _ in sides]
     outs = [refs.pop(0) for _ in sides]
-    kcat, vcat, vt = refs
+    kcat, vcat, vt, held, sems = refs
+    pairs = [(queries[n], held.at[n]) for n in range(len(sides))]
+    copies = load(pairs, sems)
     parts = []
     at = 0
     for size in (UNIT, HALF):
@@ -91,18 +119,24 @@
         at += HALF
     shared = at
     if diag:
-        kcat[at : at + ROWS, :] = own[0][...]
-        vcat[at : at + ROWS, :] = own[1][...]
+        more = load(
+            ((own[0], kcat.at[at : at + ROWS, :]), (own[1], vcat.at[at : at + ROWS, :])),
+            sems.at[len(sides) :],
+        )
+        for copy in more:
+            copy.wait()
         at += ROWS
     vt[0:HD, :] = jnp.transpose(vcat[...].astype(jnp.float32), (1, 0)).astype(jnp.bfloat16)
     vt[HD:STATE, :] = jnp.ones((STATE - HD, at), jnp.bfloat16)
 
     tiles = [(n, side, head) for n, side in enumerate(sides) for head in range(GROUP)]
+    for copy in copies:
+        copy.wait()
 
     def scores(tile):
         n, side, head = tile
         count = at if side == 0 else shared
-        query = queries[n][:, head * HD : (head + 1) * HD]
+        query = held[n, :, head * HD : (head + 1) * HD]
         return lax.dot_general(
             kcat[0:count, :], query, (((1,), (1,)), ((), ())), preferred_element_type=jnp.float32
         )
@@ -155,12 +189,16 @@
     return pl.pallas_call(
         functools.partial(attend_kernel, layouts=layouts, sides=sides, first=first, diag=diag),
         out_shape=[state] * len(sides),
-        in_specs=[smem()] + [vmem()] * (len(inputs) - 1),
+        in_specs=[smem()]
+        + [hbm()] * (len(sides) + (2 if diag else 0))
+        + [vmem()] * (len(inputs) - 1 - len(sides) - (2 if diag else 0)),
         out_specs=[vmem()] * len(sides),
         scratch_shapes=[
             pltpu.VMEM((keys, HD), jnp.bfloat16),
             pltpu.VMEM((keys, HD), jnp.bfloat16),
             pltpu.VMEM((STATE, keys), jnp.bfloat16),
+            pltpu.VMEM((len(sides), ROWS, GROUP * HD), jnp.bfloat16),
+            pltpu.SemaphoreType.DMA((len(sides) + 2,)),
         ],
         compiler_params=params(),
         cost_estimate=pl.CostEstimate(
@@ -196,51 +234,52 @@
     )(mine, theirs)
 
 
-def project_kernel(at_ref, a0, a1, a2, a3, near_ref, far_ref, near_out, far_out, far_sum):
-    step = pl.program_id(0)
-    for i, a_ref in enumerate((a0, a1, a2, a3)):
-
-        @pl.when(step == i)
-        def _(i=i, a_ref=a_ref):
-            near = jnp.dot(a_ref[...], near_ref[0, 0], preferred_element_type=jnp.float32)
-            far = jnp.dot(a_ref[...], far_ref[0, 0], preferred_element_type=jnp.float32)
-            if i == 0:
-                near_out[...] = near
-                far_sum[...] = far
-            else:
-                near_out[...] += near
-                far_sum[...] += far
-            if i == 3:
-                far_out[...] = far_sum[...].astype(jnp.bfloat16)
-
-
-def project(places, heads, weight):
-    depth, width = weight.shape[2:]
-    whole = pl.BlockSpec((ROWS, depth), lambda k, at: (0, 0))
-    result = pl.BlockSpec((ROWS, width), lambda k, at: (0, 0))
+def project_kernel(at_ref, *refs, count, side, first):
+    refs = list(refs)
+    heads = [refs.pop(0) for _ in range(count)]
+    weight = refs.pop(0)
+    start = None if first else refs.pop(0)
+    out, held, sems = refs
+    depth, width = heads[0].shape[1], held.shape[-1]
+    half = at_ref[count]
+    pairs = []
+    for i in range(count):
+        at = at_ref[i]
+        place = (half, at) if side == "near" else (1 - half, 3 - at)
+        for n in range(width // HD):
+            source = weight.at[place[0], :, place[1], n]
+            pairs.append((source, held.at[i, :, :, n * HD : (n + 1) * HD]))
+    copies = load(pairs, sems)
+    total = 0.0 if first else start[...]
+    for i in range(count):
+        for copy in copies[3 * i : 3 * i + 3]:
+            copy.wait()
+        block = held[i].reshape(depth, width)
+        total += jnp.dot(heads[i][...], block, preferred_element_type=jnp.float32)
+    out[...] = total.astype(out.dtype)
+
+
+def project(places, heads, weight, side, start=None, dtype=jnp.float32, name="project"):
+    count = len(heads)
+    shards, shard, width = weight.shape[1], weight.shape[4], weight.shape[3] * HD
+    first = start is None
     return pl.pallas_call(
-        project_kernel,
-        out_shape=[
-            jax.ShapeDtypeStruct((ROWS, width), jnp.float32),
-            jax.ShapeDtypeStruct((ROWS, width), jnp.bfloat16),
+        functools.partial(project_kernel, count=count, side=side, first=first),
+        out_shape=jax.ShapeDtypeStruct((ROWS, width), dtype),
+        in_specs=[smem()] + [vmem()] * count + [hbm()] + [vmem()] * (0 if first else 1),
+        out_specs=vmem(),
+        scratch_shapes=[
+            pltpu.VMEM((count, shards, shard, width), jnp.bfloat16),
+            pltpu.SemaphoreType.DMA((3 * count,)),
         ],
-        grid_spec=pltpu.PrefetchScalarGridSpec(
-            num_scalar_prefetch=1,
-            grid=(4,),
-            in_specs=[
-                whole,
-                whole,
-                whole,
-                whole,
-                pl.BlockSpec((1, 1, depth, width), lambda k, at: (at[k], at[4], 0, 0)),
-                pl.BlockSpec((1, 1, depth, width), lambda k, at: (3 - at[k], 1 - at[4], 0, 0)),
-            ],
-            out_specs=[result, result],
-            scratch_shapes=[pltpu.VMEM((ROWS, width), jnp.float32)],
+        compiler_params=params(),
+        cost_estimate=pl.CostEstimate(
+            flops=2 * ROWS * GROUP * HD * width * count,
+            bytes_accessed=2 * GROUP * HD * width * count,
+            transcendentals=0,
         ),
-        compiler_params=params(),
-        name="project",
-    )(places, *heads, weight, weight)
+        name=name,
+    )(places, *heads, weight, *(() if first else (start,)))
 
 
 def ring(size, distance):
@@ -252,14 +291,8 @@
     block = (y * 8 + z) * 2 + c
     swap = ring(2, 1)
 
-    anchor = jnp.concatenate([keys[HALF : 2 * HALF], values[HALF : 2 * HALF]], 0)
-    anchor = lax.ppermute(anchor, ("y", "z", "c"), [(0, 1)])
-    unit = pick(c.reshape(1), kept_rows.reshape(1, UNIT), keys, values, anchor)
-
-    came = [
-        lax.ppermute(unit, "y", [(i, i + d) for i in range(4 - d)]) for d in (1, 2, 3)
-    ]
-    other_queries = lax.ppermute(queries, "c", swap)
+    first_block = [(0, 1)]
+    anchor = [lax.ppermute(block, ("y", "z", "c"), first_block) for block in (keys, values)]
 
     pairs = []
     for yy in range(4):
@@ -267,25 +300,22 @@
             hh = 0 if zz >= 4 else 1
             pairs.append(((yy * 8 + zz) * 2 + hh, ((3 - yy) * 8 + (zz ^ 4)) * 2 + 1 - hh))
     crossed = lax.ppermute(out_weight, ("y", "z", "h"), pairs)
-    stays = (z >= 4) == (h == 1)
-    weight = lax.all_gather(
-        jnp.where(stays, out_weight, crossed), ("y", "z", "c"), axis=0, tiled=True
-    ).reshape(4, 2, 640, out_weight.shape[1])
-
-    first = functools.reduce(
-        lambda held, d: jnp.where(y == d, came[d - 1][256:384], held), (1, 2, 3), unit[256:384]
-    )
-    bundle = jnp.concatenate([unit[:256]] + [part[:256] for part in came] + [first], 0)
-
+    crossed = jnp.where((z >= 4) == (h == 1), out_weight, crossed)
+    other_queries = lax.ppermute(queries, "c", swap)
+
+    unit = pick(c.reshape(1), kept_rows.reshape(1, UNIT), keys, values, *anchor, crossed)
+    unit, other_queries = lax.optimization_barrier((unit, other_queries))
+    line = lax.all_gather(unit, "y", axis=0, tiled=False)
+    bundle = jnp.concatenate([line[:, :256].reshape(1024, HD), line[0, 256:384]], 0)
     def flags_of(source):
-        one = jnp.stack([source < z, y >= 1, y >= 2, y >= 3, source == 0])
+        one = jnp.stack([(y > i) | ((y == i) & (source < z)) for i in range(4)] + [source == 0])
         return jnp.concatenate([one, one])
 
     here = jnp.stack(
-        [
-            y < 0, y >= 1, y >= 2, y >= 3, (z == 0) & (block != 0),
-            c == 0, y >= 1, y >= 2, y >= 3, (z == 0) & (block + 1 - 2 * c != 0),
-        ]
+        [y > i for i in range(4)]
+        + [(z == 0) & (block != 0)]
+        + [(y > i) | ((y == i) & (c == 0)) for i in range(4)]
+        + [(z == 0) & (block + 1 - 2 * c != 0)]
     ).astype(jnp.int32)
 
     def flags_at(step):
@@ -297,13 +327,19 @@
     right = lax.ppermute(bundle, "z", ring(8, 1))
     left = lax.ppermute(bundle, "z", ring(8, 7))
     states = attend(here, both, [bundle], (FULL,), own=(keys, values), name="attend0")
+    rows = line[:, 384:]
     for step in (1, 2):
+        if step == WEIGHT_STEP:
+            right, left, rows, states = lax.optimization_barrier((right, left, rows, states))
         next_right = lax.ppermute(right, "z", ring(8, 1))
         next_left = lax.ppermute(left, "z", ring(8, 7))
         states = attend(
             flags_at(step), both, [right, left], (FULL, FULL), states, name=f"attend{step}"
         )
         right, left = next_right, next_left
+    if WEIGHT_STEP == 3:
+        right, rows = lax.optimization_barrier((right, rows))
+    weight = lax.all_gather(rows, ("z", "c"), axis=0, tiled=False)
     front = lax.ppermute(right[:512], "z", ring(8, 1))
     back = lax.ppermute(left[512:], "z", ring(8, 7))
     states = attend(flags_at(3), both, [right, left], (FULL, FULL), states, name="attend3")
@@ -315,10 +351,16 @@
     (mine,) = attend(flags_at(4), (queries,), *last, (states[0],), sides=(0,), name="attend4a")
     attended = merge(mine, theirs)
 
-    heads = [attended] + [lax.ppermute(attended, "x", ring(4, d)) for d in (1, 3, 2)]
-    places = jnp.stack([x, (x + 3) % 4, (x + 1) % 4, (x + 2) % 4, h]).astype(jnp.int32)
-    near, far = project(places, heads, weight)
-    return (near + lax.ppermute(far, "h", swap)).astype(jnp.bfloat16)
+    weight = weight.reshape(2, 8, 4, 3, out_weight.shape[0], HD)
+    nearby = jnp.stack([x, h]).astype(jnp.int32)
+    across = jnp.stack([(x + 3) % 4, (x + 1) % 4, (x + 2) % 4, h]).astype(jnp.int32)
+    gathered = [lax.ppermute(attended, "x", ring(4, d)) for d in (1, 3, 2)]
+    far = project(nearby, [attended], weight, "far", name="far0")
+    near = project(nearby, [attended], weight, "near", name="near0")
+    far = project(across, gathered, weight, "far", far, jnp.bfloat16, name="far1")
+    crossing = lax.ppermute(far, "h", swap)
+    near = project(across, gathered, weight, "near", near, name="near1")
+    return (near + crossing).astype(jnp.bfloat16)
 
 
 def solution(mesh):

time: 175 us -> 160 us (0.914)
  the two profiles are of different devices: /device:TPU:40 before, /device:TPU:2 now
where the time goes in v2:
time: 160 us; the launch traced here: 159 us
  starting transfers between devices  60.6 us (38%)
  Pallas kernels  30.8 us (19%)
  waiting for transfers between devices  25.2 us (16%)
  blocking collectives  18.3 us (11%)
  between operations  14.1 us (9%)
  local copies, waits for them, and re-layouts  8.47 us (5%)
  other arithmetic  1.77 us (1%)
    pallas_call x6, Pallas kernels, attend(): pl.pallas_call(functools.partial(attend_kernel, layouts=layouts, sides=si...  24.4 us
    all_gather x1, blocking collectives, local(): line = lax.all_gather(unit, 'y', axis=0, tiled=False)  18.3 us
    ppermute x1, starting transfers between devices, local(): left = lax.ppermute(bundle, 'z', ring(8, 7))  17.9 us
    ppermute x1, waiting for transfers between devices, local(): crossing = lax.ppermute(far, 'h', swap)  10.9 us
    ppermute x3, waiting for transfers between devices, local(): gathered = [lax.ppermute(attended, 'x', ring(4, d)) for d in (1, 3, 2)]  9.56 us
    ppermute x3, starting transfers between devices, local(): gathered = [lax.ppermute(attended, 'x', ring(4, d)) for d in (1, 3, 2)]  9.26 us
    ppermute x2, starting transfers between devices, local(): next_left = lax.ppermute(left, 'z', ring(8, 7))  9.04 us
    unnamed x18, local copies, waits for them, and re-layouts  7.11 us
  transfers between devices with their start and end apart: 18, of which 6 were waited for; matrix products, arithmetic and copies ran while one was open for 1% of the time, Pallas kernels for 18%

profile of v2, /device:TPU:2, one launch (start us, length us, event | category | flops | bytes accessed | tf_op | source)
XLA Modules:
  0.0 159.2 jit_solution(16263293329321272322)
XLA Ops:
  6.5 1.9 %collective-permute-start.3 = (bf16[256,640]{1,0:T(8,128)(2,1)}, bf16[256,640]{1,0:T(8,128)(2,1)S(1)}, u32[]{:S(2)}, u32[]{:S(2)}) collective-permute-start(bf16[256,640]{1,0:T(8,128)(2,1)} %refs_1_.9), channel_id=1, source_target_pairs={{0,8},{8,0},{1,9},{9,1},{2,10},{10,2},{3,11},{11,3},{4,12},{12,4},... | collective-permute-start | bytes 983048 | tf_op jit(solution)/shard_map/ppermute | solution.py:304
  8.5 0.7 collective-permute-start.2
  9.1 2.4 %collective-permute-start = (bf16[256,128]{1,0:T(8,128)(2,1)}, bf16[256,128]{1,0:T(8,128)(2,1)S(1)}, u32[]{:S(2)}, u32[]{:S(2)}) collective-permute-start(bf16[256,128]{1,0:T(8,128)(2,1)} %refs_3_.1), channel_id=1, source_target_pairs={{0,8},{1,9},{2,10},{3,11},{4,12},{5,13},{6,14},{7,15}} | collective-permute-start | bytes 196616 | tf_op jit(solution)/shard_map/ppermute | solution.py:295
  11.5 1.3 collective-permute-start.1
  12.9 0.8 broadcast_select_fusion.weight_ref
  13.7 0.2 collective-permute-done.1.far_vals
  13.9 0.8 copy-done.2
  14.8 0.8 copy-done.4
  15.6 0.7 copy-done.6
  16.3 0.4 pick.1
  16.7 18.3 %all-gather = bf16[2496,128]{1,0:T(8,128)(2,1)S(1)} all-gather(bf16[624,128]{1,0:T(8,128)(2,1)S(1)} %pick.1), channel_id=2, replica_groups=mesh['y'=4,'z'=8,'c'=2,'x'=4,'h'=2] {'y'}, dimensions={0}, use_global_device_ids=true | all-gather | bytes 798720 | tf_op jit(solution)/shard_map/all_gather | solution.py:308
  35.1 2.9 %collective-permute-start.4 = (bf16[1152,128]{1,0:T(8,128)(2,1)S(1)}, bf16[1152,128]{1,0:T(8,128)(2,1)S(1)}, u32[]{:S(2)}, u32[]{:S(2)}) collective-permute-start(bf16[1152,128]{1,0:T(8,128)(2,1)S(1)} %pad_maximum_fusion.refs_5_), channel_id=1, source_target_pairs={{0,16},{16,32},{32,48},{48,64},{64,80},{80,96},{96,112},{112,0},{1... | collective-permute-start | bytes 884744 | tf_op jit(solution)/shard_map/ppermute | solution.py:327
  38.0 17.9 %collective-permute-start.5 = (bf16[1152,128]{1,0:T(8,128)(2,1)S(1)}, bf16[1152,128]{1,0:T(8,128)(2,1)S(1)}, u32[]{:S(2)}, u32[]{:S(2)}) collective-permute-start(bf16[1152,128]{1,0:T(8,128)(2,1)S(1)} %pad_maximum_fusion.refs_5_), channel_id=1, source_target_pairs={{0,112},{16,0},{32,16},{48,32},{64,48},{80,64},{96,80},{112,96},{1... | collective-permute-start | bytes 884744 | tf_op jit(solution)/shard_map/ppermute | solution.py:328
  56.1 0.7 slice.22
  56.8 0.8 copy-done.3
  57.7 0.8 copy-done.5
  58.5 1.0 copy-done.7
  59.5 4.1 %attend0.1 = (f32[5,144,256]{2,1,0:T(8,128)S(1)}, f32[5,144,256]{2,1,0:T(8,128)S(1)}) custom-call(s32[10]{0:T(128)S(1)} %convert_element_type.23.refs_0_, bf16[256,640]{1,0:T(8,128)(2,1)S(1)} %copy-done.7, bf16[256,640]{1,0:T(8,128)(2,1)S(1)} %collective-permute-done.3.refs_2_.refs_1_, bf16[256,128]{1,0:T(8,128)(2,1)S(1)} %copy-done.3, ...), custom_call_target="tpu_custom_call" | custom-call | flops 2348810240 | bytes 4194304 | tf_op jit(solution)/shard_map/attend0/pallas_call | solution.py:189
  63.6 3.9 %collective-permute-start.9 = (bf16[1152,128]{1,0:T(8,128)(2,1)S(1)}, bf16[1152,128]{1,0:T(8,128)(2,1)S(1)}, u32[]{:S(2)}, u32[]{:S(2)}) collective-permute-start(bf16[1152,128]{1,0:T(8,128)(2,1)S(1)} %collective-permute-done.5.refs_4_), channel_id=1, source_target_pairs={{0,112},{16,0},{32,16},{48,32},{64,48},{80,64},{96,80},{112,96},{1... | collective-permute-start | bytes 884744 | tf_op jit(solution)/shard_map/ppermute | solution.py:335
  67.5 1.9 %collective-permute-start.6 = (bf16[1152,128]{1,0:T(8,128)(2,1)S(1)}, bf16[1152,128]{1,0:T(8,128)(2,1)S(1)}, u32[]{:S(2)}, u32[]{:S(2)}) collective-permute-start(bf16[1152,128]{1,0:T(8,128)(2,1)S(1)} %collective-permute-done.4.refs_3_), channel_id=1, source_target_pairs={{0,16},{16,32},{32,48},{48,64},{64,80},{80,96},{96,112},{112,0},{1... | collective-permute-start | bytes 884744 | tf_op jit(solution)/shard_map/ppermute | solution.py:334
  69.8 0.1 concatenate.24
  70.0 0.1 concatenate.23
  70.2 2.0 %collective-permute-done.9.refs_4_ = bf16[1152,128]{1,0:T(8,128)(2,1)S(1)} collective-permute-done((bf16[1152,128]{1,0:T(8,128)(2,1)S(1)}, bf16[1152,128]{1,0:T(8,128)(2,1)S(1)}, u32[]{:S(2)}, u32[]{:S(2)}) %collective-permute-start.9) | collective-permute-done | bytes 294944 | tf_op jit(solution)/shard_map/ppermute | solution.py:335
  72.2 5.1 %collective-permute-start.10 = (bf16[1152,128]{1,0:T(8,128)(2,1)S(1)}, bf16[1152,128]{1,0:T(8,128)(2,1)S(1)}, u32[]{:S(2)}, u32[]{:S(2)}) collective-permute-start(bf16[1152,128]{1,0:T(8,128)(2,1)S(1)} %collective-permute-done.9.refs_4_), channel_id=1, source_target_pairs={{0,112},{16,0},{32,16},{48,32},{64,48},{80,64},{96,80},{112,96},{1... | collective-permute-start | bytes 884744 | tf_op jit(solution)/shard_map/ppermute | solution.py:335
  77.3 2.1 %collective-permute-start.7 = (bf16[1152,128]{1,0:T(8,128)(2,1)S(1)}, bf16[1152,128]{1,0:T(8,128)(2,1)S(1)}, u32[]{:S(2)}, u32[]{:S(2)}) collective-permute-start(bf16[1152,128]{1,0:T(8,128)(2,1)S(1)} %collective-permute-done.6.refs_3_), channel_id=1, source_target_pairs={{0,16},{16,32},{32,48},{48,64},{64,80},{80,96},{96,112},{112,0},{1... | collective-permute-start | bytes 884744 | tf_op jit(solution)/shard_map/ppermute | solution.py:334
  79.5 5.3 %attend1.1 = (f32[5,144,256]{2,1,0:T(8,128)S(1)}, f32[5,144,256]{2,1,0:T(8,128)S(1)}) custom-call(s32[20]{0:T(128)S(1)} %convert_element_type.26.refs_0_, bf16[256,640]{1,0:T(8,128)(2,1)S(1)} %copy-done.8, bf16[256,640]{1,0:T(8,128)(2,1)S(1)} %collective-permute-done.3.refs_2_.refs_1_, bf16[1152,128]{1,0:T(8,128)(2,1)S(1)} %collective-permute-done.4.refs_3_, ...), custom_call_target="tpu_custom_call" | custom-call | flops 3019898880 | bytes 4194304 | tf_op jit(solution)/shard_map/attend1/pallas_call | solution.py:189
  84.8 5.3 %attend2.1 = (f32[5,144,256]{2,1,0:T(8,128)S(1)}, f32[5,144,256]{2,1,0:T(8,128)S(1)}) custom-call(s32[20]{0:T(128)S(1)} %convert_element_type.25.refs_0_, bf16[256,640]{1,0:T(8,128)(2,1)S(1)} %copy-done.8, bf16[256,640]{1,0:T(8,128)(2,1)S(1)} %collective-permute-done.3.refs_2_.refs_1_, bf16[1152,128]{1,0:T(8,128)(2,1)S(1)} %collective-permute-done.6.refs_3_, ...), custom_call_target="tpu_custom_call" | custom-call | flops 3019898880 | bytes 4194304 | tf_op jit(solution)/shard_map/attend2/pallas_call | solution.py:189
  90.2 5.1 %collective-permute-start.11 = (bf16[640,128]{1,0:T(8,128)(2,1)S(1)}, bf16[640,128]{1,0:T(8,128)(2,1)S(1)}, u32[]{:S(2)}, u32[]{:S(2)}) collective-permute-start(bf16[640,128]{1,0:T(8,128)(2,1)S(1)} %slice.24), channel_id=1, source_target_pairs={{0,112},{16,0},{32,16},{48,32},{64,48},{80,64},{96,80},{112,96},{1... | collective-permute-start | bytes 491528 | tf_op jit(solution)/shard_map/ppermute | solution.py:344
  95.3 2.1 %collective-permute-start.8 = (bf16[512,128]{1,0:T(8,128)(2,1)S(1)}, bf16[512,128]{1,0:T(8,128)(2,1)S(1)}, u32[]{:S(2)}, u32[]{:S(2)}) collective-permute-start(bf16[512,128]{1,0:T(8,128)(2,1)S(1)} %slice.23), channel_id=1, source_target_pairs={{0,16},{16,32},{32,48},{48,64},{64,80},{80,96},{96,112},{112,0},{1... | collective-permute-start | bytes 393224 | tf_op jit(solution)/shard_map/ppermute | solution.py:343
  97.5 5.3 %attend3.1 = (f32[5,144,256]{2,1,0:T(8,128)S(1)}, f32[5,144,256]{2,1,0:T(8,128)S(1)}) custom-call(s32[20]{0:T(128)S(1)} %convert_element_type.24.refs_0_, bf16[256,640]{1,0:T(8,128)(2,1)S(1)} %copy-done.8, bf16[256,640]{1,0:T(8,128)(2,1)S(1)} %collective-permute-done.3.refs_2_.refs_1_, bf16[1152,128]{1,0:T(8,128)(2,1)S(1)} %collective-permute-done.7.refs_3_, ...), custom_call_target="tpu_custom_call" | custom-call | flops 3019898880 | bytes 4194304 | tf_op jit(solution)/shard_map/attend3/pallas_call | solution.py:189
  102.8 2.6 %collective-permute-done.8.refs_2_ = bf16[512,128]{1,0:T(8,128)(2,1)S(1)} collective-permute-done((bf16[512,128]{1,0:T(8,128)(2,1)S(1)}, bf16[512,128]{1,0:T(8,128)(2,1)S(1)}, u32[]{:S(2)}, u32[]{:S(2)}) %collective-permute-start.8) | collective-permute-done | bytes 131104 | tf_op jit(solution)/shard_map/ppermute | solution.py:343
  105.4 2.2 %attend4b.1 = f32[5,144,256]{2,1,0:T(8,128)S(1)} custom-call(s32[20]{0:T(128)S(1)} %convert_element_type.22.refs_0_, bf16[256,640]{1,0:T(8,128)(2,1)S(1)} %collective-permute-done.3.refs_2_.refs_1_, bf16[512,128]{1,0:T(8,128)(2,1)S(1)} %collective-permute-done.8.refs_2_, bf16[640,128]{1,0:T(8,128)(2,1)S(1)} %collective-permute-done.11.refs_3_, ...), custom_call_target="tpu_custom_call" | custom-call | flops 838860800 | bytes 4194304 | tf_op jit(solution)/shard_map/attend4b/pallas_call | solution.py:189
  107.6 1.9 %collective-permute-start.12 = (f32[5,144,256]{2,1,0:T(8,128)S(1)}, f32[5,144,256]{2,1,0:T(8,128)S(1)}, u32[]{:S(2)}, u32[]{:S(2)}) collective-permute-start(f32[5,144,256]{2,1,0:T(8,128)S(1)} %attend4b.1), channel_id=1, source_target_pairs={{0,8},{8,0},{1,9},{9,1},{2,10},{10,2},{3,11},{11,3},{4,12},{12,4},... | collective-permute-start | bytes 2211848 | tf_op jit(solution)/shard_map/ppermute | solution.py:350
  109.5 2.2 %attend4a.1.mine_ref = f32[5,144,256]{2,1,0:T(8,128)S(1)} custom-call(s32[20]{0:T(128)S(1)} %convert_element_type.22.refs_0_, bf16[256,640]{1,0:T(8,128)(2,1)S(1)} %copy-done.8, bf16[512,128]{1,0:T(8,128)(2,1)S(1)} %collective-permute-done.8.refs_2_, bf16[640,128]{1,0:T(8,128)(2,1)S(1)} %collective-permute-done.11.refs_3_, ...), custom_call_target="tpu_custom_call" | custom-call | flops 838860800 | bytes 4194304 | tf_op jit(solution)/shard_map/attend4a/pallas_call | solution.py:189
  111.7 0.2 merge.1.refs_0_
  111.9 3.4 %collective-permute-start.13 = (bf16[256,640]{1,0:T(8,128)(2,1)S(1)}, bf16[256,640]{1,0:T(8,128)(2,1)S(1)}, u32[]{:S(2)}, u32[]{:S(2)}) collective-permute-start(bf16[256,640]{1,0:T(8,128)(2,1)S(1)} %merge.1.refs_0_), channel_id=1, source_target_pairs={{0,2},{2,4},{4,6},{6,0},{1,3},{3,5},{5,7},{7,1},{8,10},{10,12},{12... | collective-permute-start | bytes 983048 | tf_op jit(solution)/shard_map/ppermute | solution.py:357
  115.3 2.5 %collective-permute-start.14 = (bf16[256,640]{1,0:T(8,128)(2,1)S(1)}, bf16[256,640]{1,0:T(8,128)(2,1)S(1)}, u32[]{:S(2)}, u32[]{:S(2)}) collective-permute-start(bf16[256,640]{1,0:T(8,128)(2,1)S(1)} %merge.1.refs_0_), channel_id=1, source_target_pairs={{0,6},{2,0},{4,2},{6,4},{1,7},{3,1},{5,3},{7,5},{8,14},{10,8},{12,... | collective-permute-start | bytes 983048 | tf_op jit(solution)/shard_map/ppermute | solution.py:357
  117.8 3.4 %collective-permute-start.15 = (bf16[256,640]{1,0:T(8,128)(2,1)S(1)}, bf16[256,640]{1,0:T(8,128)(2,1)S(1)}, u32[]{:S(2)}, u32[]{:S(2)}) collective-permute-start(bf16[256,640]{1,0:T(8,128)(2,1)S(1)} %merge.1.refs_0_), channel_id=1, source_target_pairs={{0,4},{2,6},{4,0},{6,2},{1,5},{3,7},{5,1},{7,3},{8,12},{10,14},{12... | collective-permute-start | bytes 983048 | tf_op jit(solution)/shard_map/ppermute | solution.py:357
  121.4 2.1 %copy-done = bf16[64,240,128]{2,1,0:T(8,128)(2,1)S(1)} copy-done((bf16[64,240,128]{2,1,0:T(8,128)(2,1)S(1)}, bf16[64,240,128]{2,1,0:T(8,128)(2,1)}, u32[]{:S(2)}) %copy-start) | copy-done | bytes 3932184
  123.5 1.0 far0.1.refs_4_
  124.5 3.1 %collective-permute-done.14.refs_1_ = bf16[256,640]{1,0:T(8,128)(2,1)S(1)} collective-permute-done((bf16[256,640]{1,0:T(8,128)(2,1)S(1)}, bf16[256,640]{1,0:T(8,128)(2,1)S(1)}, u32[]{:S(2)}, u32[]{:S(2)}) %collective-permute-start.14) | collective-permute-done | bytes 327712 | tf_op jit(solution)/shard_map/ppermute | solution.py:357
  127.6 6.5 %collective-permute-done.15.refs_2_ = bf16[256,640]{1,0:T(8,128)(2,1)S(1)} collective-permute-done((bf16[256,640]{1,0:T(8,128)(2,1)S(1)}, bf16[256,640]{1,0:T(8,128)(2,1)S(1)}, u32[]{:S(2)}, u32[]{:S(2)}) %collective-permute-start.15) | collective-permute-done | bytes 327712 | tf_op jit(solution)/shard_map/ppermute | solution.py:357
  134.1 1.9 %far1.1 = bf16[256,384]{1,0:T(8,128)(2,1)S(1)} custom-call(s32[4]{0:T(128)S(1)} %pad_add_fusion.at_ref, bf16[256,640]{1,0:T(8,128)(2,1)S(1)} %collective-permute-done.13.refs_0_, bf16[256,640]{1,0:T(8,128)(2,1)S(1)} %collective-permute-done.14.refs_1_, bf16[256,640]{1,0:T(8,128)(2,1)S(1)} %collective-permute-done.15.refs_2_, ...), custom_call_target="tpu_custom_call" | custom-call | flops 377487360 | bytes 1474560 | tf_op jit(solution)/shard_map/far1/pallas_call | solution.py:266
  136.0 1.9 %collective-permute-start.16 = (bf16[256,384]{1,0:T(8,128)(2,1)S(1)}, bf16[256,384]{1,0:T(8,128)(2,1)S(1)}, u32[]{:S(2)}, u32[]{:S(2)}) collective-permute-start(bf16[256,384]{1,0:T(8,128)(2,1)S(1)} %far1.1), channel_id=1, source_target_pairs={{0,1},{1,0},{2,3},{3,2},{4,5},{5,4},{6,7},{7,6},{8,9},{9,8},{10,11... | collective-permute-start | bytes 589832 | tf_op jit(solution)/shard_map/ppermute | solution.py:361
  137.9 1.0 near0.1.refs_4_
  138.9 1.9 %near1.1 = f32[256,384]{1,0:T(8,128)S(1)} custom-call(s32[4]{0:T(128)S(1)} %pad_add_fusion.at_ref, bf16[256,640]{1,0:T(8,128)(2,1)S(1)} %collective-permute-done.13.refs_0_, bf16[256,640]{1,0:T(8,128)(2,1)S(1)} %collective-permute-done.14.refs_1_, bf16[256,640]{1,0:T(8,128)(2,1)S(1)} %collective-permute-done.15.refs_2_, ...), custom_call_target="tpu_custom_call" | custom-call | flops 377487360 | bytes 1474560 | tf_op jit(solution)/shard_map/near1/pallas_call | solution.py:266
  140.8 10.9 %collective-permute-done.16 = bf16[256,384]{1,0:T(8,128)(2,1)S(1)} collective-permute-done((bf16[256,384]{1,0:T(8,128)(2,1)S(1)}, bf16[256,384]{1,0:T(8,128)(2,1)S(1)}, u32[]{:S(2)}, u32[]{:S(2)}) %collective-permute-start.16) | collective-permute-done | bytes 196640 | tf_op jit(solution)/shard_map/ppermute | solution.py:361
  151.6 0.7 add_convert_fusion
  (40 shorter events, 0.7 us)
Async XLA Ops:
  6.5 114.9 %all-gather.4.cloned.1.call-start = ((), (), s32[]{:S(2)}) async-start(), calls=%async_computation | async-start | bytes 4177920 | tf_op jit(solution)/shard_map/all_gather | solution.py:342
  6.5 10.2 %collective-permute-start.3 = (bf16[256,640]{1,0:T(8,128)(2,1)}, bf16[256,640]{1,0:T(8,128)(2,1)S(1)}, u32[]{:S(2)}, u32[]{:S(2)}) collective-permute-start(bf16[256,640]{1,0:T(8,128)(2,1)} %refs_1_.9), channel_id=1, source_target_pairs={{0,8},{8,0},{1,9},{9,1},{2,10},{10,2},{3,11},{11,3},{4,12},{12,4},... | collective-permute-start | bytes 983048 | tf_op jit(solution)/shard_map/ppermute | solution.py:304
  8.5 4.4 %collective-permute-start.2 = (bf16[80,384]{1,0:T(8,128)(2,1)}, bf16[80,384]{1,0:T(8,128)(2,1)S(1)}, u32[]{:S(2)}, u32[]{:S(2)}) collective-permute-start(bf16[80,384]{1,0:T(8,128)(2,1)} %param.9), channel_id=1, source_target_pairs={{1,448},{17,464},{33,480},{49,496},{64,385},{80,401},{96,417},{112... | collective-permute-start | bytes 184328 | tf_op jit(solution)/shard_map/ppermute | solution.py:302
  9.1 4.6 %collective-permute-start = (bf16[256,128]{1,0:T(8,128)(2,1)}, bf16[256,128]{1,0:T(8,128)(2,1)S(1)}, u32[]{:S(2)}, u32[]{:S(2)}) collective-permute-start(bf16[256,128]{1,0:T(8,128)(2,1)} %refs_3_.1), channel_id=1, source_target_pairs={{0,8},{1,9},{2,10},{3,11},{4,12},{5,13},{6,14},{7,15}} | collective-permute-start | bytes 196616 | tf_op jit(solution)/shard_map/ppermute | solution.py:295
  11.5 2.4 %collective-permute-start.1 = (bf16[256,128]{1,0:T(8,128)(2,1)}, bf16[256,128]{1,0:T(8,128)(2,1)S(1)}, u32[]{:S(2)}, u32[]{:S(2)}) collective-permute-start(bf16[256,128]{1,0:T(8,128)(2,1)} %refs_4_.1), channel_id=1, source_target_pairs={{0,8},{1,9},{2,10},{3,11},{4,12},{5,13},{6,14},{7,15}} | collective-permute-start | bytes 196616 | tf_op jit(solution)/shard_map/ppermute | solution.py:295
  13.9 0.8 copy-start.2
  14.8 0.8 copy-start.4
  15.6 0.7 copy-start.6
  35.1 28.5 %collective-permute-start.4 = (bf16[1152,128]{1,0:T(8,128)(2,1)S(1)}, bf16[1152,128]{1,0:T(8,128)(2,1)S(1)}, u32[]{:S(2)}, u32[]{:S(2)}) collective-permute-start(bf16[1152,128]{1,0:T(8,128)(2,1)S(1)} %pad_maximum_fusion.refs_5_), channel_id=1, source_target_pairs={{0,16},{16,32},{32,48},{48,64},{64,80},{80,96},{96,112},{112,0},{1... | collective-permute-start | bytes 884744 | tf_op jit(solution)/shard_map/ppermute | solution.py:327
  38.0 25.6 %collective-permute-start.5 = (bf16[1152,128]{1,0:T(8,128)(2,1)S(1)}, bf16[1152,128]{1,0:T(8,128)(2,1)S(1)}, u32[]{:S(2)}, u32[]{:S(2)}) collective-permute-start(bf16[1152,128]{1,0:T(8,128)(2,1)S(1)} %pad_maximum_fusion.refs_5_), channel_id=1, source_target_pairs={{0,112},{16,0},{32,16},{48,32},{64,48},{80,64},{96,80},{112,96},{1... | collective-permute-start | bytes 884744 | tf_op jit(solution)/shard_map/ppermute | solution.py:328
  56.8 0.8 copy-start.3
  57.7 0.8 copy-start.5
  58.5 1.0 copy-start.7
  59.5 20.0 %copy-start.8 = (bf16[256,640]{1,0:T(8,128)(2,1)S(1)}, bf16[256,640]{1,0:T(8,128)(2,1)}, u32[]{:S(2)}) copy-start(bf16[256,640]{1,0:T(8,128)(2,1)} %refs_1_.9) | copy-start | bytes 983044
  63.6 8.6 %collective-permute-start.9 = (bf16[1152,128]{1,0:T(8,128)(2,1)S(1)}, bf16[1152,128]{1,0:T(8,128)(2,1)S(1)}, u32[]{:S(2)}, u32[]{:S(2)}) collective-permute-start(bf16[1152,128]{1,0:T(8,128)(2,1)S(1)} %collective-permute-done.5.refs_4_), channel_id=1, source_target_pairs={{0,112},{16,0},{32,16},{48,32},{64,48},{80,64},{96,80},{112,96},{1... | collective-permute-start | bytes 884744 | tf_op jit(solution)/shard_map/ppermute | solution.py:335
  67.5 9.8 %collective-permute-start.6 = (bf16[1152,128]{1,0:T(8,128)(2,1)S(1)}, bf16[1152,128]{1,0:T(8,128)(2,1)S(1)}, u32[]{:S(2)}, u32[]{:S(2)}) collective-permute-start(bf16[1152,128]{1,0:T(8,128)(2,1)S(1)} %collective-permute-done.4.refs_3_), channel_id=1, source_target_pairs={{0,16},{16,32},{32,48},{48,64},{64,80},{80,96},{96,112},{112,0},{1... | collective-permute-start | bytes 884744 | tf_op jit(solution)/shard_map/ppermute | solution.py:334
  72.2 17.9 %collective-permute-start.10 = (bf16[1152,128]{1,0:T(8,128)(2,1)S(1)}, bf16[1152,128]{1,0:T(8,128)(2,1)S(1)}, u32[]{:S(2)}, u32[]{:S(2)}) collective-permute-start(bf16[1152,128]{1,0:T(8,128)(2,1)S(1)} %collective-permute-done.9.refs_4_), channel_id=1, source_target_pairs={{0,112},{16,0},{32,16},{48,32},{64,48},{80,64},{96,80},{112,96},{1... | collective-permute-start | bytes 884744 | tf_op jit(solution)/shard_map/ppermute | solution.py:335
  77.3 18.0 %collective-permute-start.7 = (bf16[1152,128]{1,0:T(8,128)(2,1)S(1)}, bf16[1152,128]{1,0:T(8,128)(2,1)S(1)}, u32[]{:S(2)}, u32[]{:S(2)}) collective-permute-start(bf16[1152,128]{1,0:T(8,128)(2,1)S(1)} %collective-permute-done.6.refs_3_), channel_id=1, source_target_pairs={{0,16},{16,32},{32,48},{48,64},{64,80},{80,96},{96,112},{112,0},{1... | collective-permute-start | bytes 884744 | tf_op jit(solution)/shard_map/ppermute | solution.py:334
  90.2 15.2 %collective-permute-start.11 = (bf16[640,128]{1,0:T(8,128)(2,1)S(1)}, bf16[640,128]{1,0:T(8,128)(2,1)S(1)}, u32[]{:S(2)}, u32[]{:S(2)}) collective-permute-start(bf16[640,128]{1,0:T(8,128)(2,1)S(1)} %slice.24), channel_id=1, source_target_pairs={{0,112},{16,0},{32,16},{48,32},{64,48},{80,64},{96,80},{112,96},{1... | collective-permute-start | bytes 491528 | tf_op jit(solution)/shard_map/ppermute | solution.py:344
  95.3 10.0 %collective-permute-start.8 = (bf16[512,128]{1,0:T(8,128)(2,1)S(1)}, bf16[512,128]{1,0:T(8,128)(2,1)S(1)}, u32[]{:S(2)}, u32[]{:S(2)}) collective-permute-start(bf16[512,128]{1,0:T(8,128)(2,1)S(1)} %slice.23), channel_id=1, source_target_pairs={{0,16},{16,32},{32,48},{48,64},{64,80},{80,96},{96,112},{112,0},{1... | collective-permute-start | bytes 393224 | tf_op jit(solution)/shard_map/ppermute | solution.py:343
  107.6 4.1 %collective-permute-start.12 = (f32[5,144,256]{2,1,0:T(8,128)S(1)}, f32[5,144,256]{2,1,0:T(8,128)S(1)}, u32[]{:S(2)}, u32[]{:S(2)}) collective-permute-start(f32[5,144,256]{2,1,0:T(8,128)S(1)} %attend4b.1), channel_id=1, source_target_pairs={{0,8},{8,0},{1,9},{9,1},{2,10},{10,2},{3,11},{11,3},{4,12},{12,4},... | collective-permute-start | bytes 2211848 | tf_op jit(solution)/shard_map/ppermute | solution.py:350
  111.9 12.6 %collective-permute-start.13 = (bf16[256,640]{1,0:T(8,128)(2,1)S(1)}, bf16[256,640]{1,0:T(8,128)(2,1)S(1)}, u32[]{:S(2)}, u32[]{:S(2)}) collective-permute-start(bf16[256,640]{1,0:T(8,128)(2,1)S(1)} %merge.1.refs_0_), channel_id=1, source_target_pairs={{0,2},{2,4},{4,6},{6,0},{1,3},{3,5},{5,7},{7,1},{8,10},{10,12},{12... | collective-permute-start | bytes 983048 | tf_op jit(solution)/shard_map/ppermute | solution.py:357
  115.3 12.4 %collective-permute-start.14 = (bf16[256,640]{1,0:T(8,128)(2,1)S(1)}, bf16[256,640]{1,0:T(8,128)(2,1)S(1)}, u32[]{:S(2)}, u32[]{:S(2)}) collective-permute-start(bf16[256,640]{1,0:T(8,128)(2,1)S(1)} %merge.1.refs_0_), channel_id=1, source_target_pairs={{0,6},{2,0},{4,2},{6,4},{1,7},{3,1},{5,3},{7,5},{8,14},{10,8},{12,... | collective-permute-start | bytes 983048 | tf_op jit(solution)/shard_map/ppermute | solution.py:357
  117.8 16.3 %collective-permute-start.15 = (bf16[256,640]{1,0:T(8,128)(2,1)S(1)}, bf16[256,640]{1,0:T(8,128)(2,1)S(1)}, u32[]{:S(2)}, u32[]{:S(2)}) collective-permute-start(bf16[256,640]{1,0:T(8,128)(2,1)S(1)} %merge.1.refs_0_), channel_id=1, source_target_pairs={{0,4},{2,6},{4,0},{6,2},{1,5},{3,7},{5,1},{7,3},{8,12},{10,14},{12... | collective-permute-start | bytes 983048 | tf_op jit(solution)/shard_map/ppermute | solution.py:357
  121.4 2.1 %copy-start = (bf16[64,240,128]{2,1,0:T(8,128)(2,1)S(1)}, bf16[64,240,128]{2,1,0:T(8,128)(2,1)}, u32[]{:S(2)}) copy-start(bf16[64,240,128]{2,1,0:T(8,128)(2,1)} %all-gather.4.cloned.1.call-done) | copy-start | bytes 11796484
  123.5 10.6 %copy-start.1 = (bf16[64,240,128]{2,1,0:T(8,128)(2,1)S(1)}, bf16[64,240,128]{2,1,0:T(8,128)(2,1)}, u32[]{:S(2)}) copy-start(bf16[64,240,128]{2,1,0:T(8,128)(2,1)} %all-gather.4.cloned.1.call-done) | copy-start | bytes 11796484
  136.0 15.7 %collective-permute-start.16 = (bf16[256,384]{1,0:T(8,128)(2,1)S(1)}, bf16[256,384]{1,0:T(8,128)(2,1)S(1)}, u32[]{:S(2)}, u32[]{:S(2)}) collective-permute-start(bf16[256,384]{1,0:T(8,128)(2,1)S(1)} %far1.1), channel_id=1, source_target_pairs={{0,1},{1,0},{2,3},{3,2},{4,5},{5,4},{6,7},{7,6},{8,9},{9,8},{10,11... | collective-permute-start | bytes 589832 | tf_op jit(solution)/shard_map/ppermute | solution.py:361
Sparse Core Ops, SparseCore 0:
  63.7 44.0 all-gather.3

commit v3 on v2

--- a/solution.py
+++ b/solution.py
@@ -16,6 +16,7 @@
 MASKED = -1e30
 SCALE = HD**-0.5 * 1.4426950408889634
 STATE = HD + 16
+FAR = 40.0
 WEIGHT_STEP = 1
 VMEM = 20 * 1024 * 1024
 
@@ -141,7 +142,7 @@
             kcat[0:count, :], query, (((1,), (1,)), ((), ())), preferred_element_type=jnp.float32
         )
 
-    def finish(tile, raw):
+    def finish(tile, raw, exact):
         n, side, head = tile
         count = at if side == 0 else shared
         pieces = []
@@ -156,26 +157,57 @@
             key_at = lax.broadcasted_iota(jnp.int32, (ROWS, ROWS), 0)
             row_at = lax.broadcasted_iota(jnp.int32, (ROWS, ROWS), 1)
             pieces.append(jnp.where(key_at <= row_at, raw[shared:at, :], MASKED))
-        top = functools.reduce(
-            jnp.maximum, [jnp.max(piece, axis=0, keepdims=True) for piece in pieces]
-        )
-        if not first:
-            old_top = states[n][head, HD + 8 : HD + 9, :]
-            top = jnp.maximum(top, old_top)
+        if exact:
+            top = functools.reduce(
+                jnp.maximum, [jnp.max(piece, axis=0, keepdims=True) for piece in pieces]
+            )
+            if not first:
+                old_top = states[n][head, HD + 8 : HD + 9, :]
+                old_top = jnp.where(states[n][head, HD : HD + 1, :] > 0.0, old_top, MASKED)
+                top = jnp.maximum(top, old_top)
+            elif side == 1:
+                some = jnp.max(raw[0:8, :], axis=0, keepdims=True)
+                top = jnp.where(top > 0.5 * MASKED, top, some)
+        else:
+            top = states[n][head, HD + 8 : HD + 9, :]
+        above = [piece - top for piece in pieces]
         weights = jnp.concatenate(
-            [jnp.exp2((piece - top) * SCALE).astype(jnp.bfloat16) for piece in pieces], 0
+            [jnp.exp2(piece * SCALE).astype(jnp.bfloat16) for piece in above], 0
         )
         total = jnp.dot(vt[:, 0:count], weights, preferred_element_type=jnp.float32)
         if not first:
-            total = total + states[n][head] * jnp.exp2((old_top - top) * SCALE)
+            held_sum = states[n][head]
+            total = total + (held_sum * jnp.exp2((old_top - top) * SCALE) if exact else held_sum)
         outs[n][head, 0 : HD + 8, :] = total[0 : HD + 8, :]
         outs[n][head, HD + 8 : STATE, :] = jnp.broadcast_to(top, (8, ROWS))
-
-    raw = scores(tiles[0])
-    for i, tile in enumerate(tiles):
-        following = scores(tiles[i + 1]) if i + 1 < len(tiles) else None
-        finish(tile, raw)
-        raw = following
+        if exact:
+            return None
+        folded = [jnp.max(piece.reshape(-1, 8, ROWS), axis=0) for piece in above]
+        most = jnp.max(functools.reduce(jnp.maximum, folded), axis=0, keepdims=True)
+        if side == 0:
+            return most
+        low = (held_sum[HD : HD + 1, :] == 0.0) & (most * SCALE < -FAR) & (most > 0.5 * MASKED)
+        return jnp.where(low, -MASKED, most)
+
+    def work(exact):
+        highest = None
+        raw = scores(tiles[0])
+        for i, tile in enumerate(tiles):
+            following = scores(tiles[i + 1]) if i + 1 < len(tiles) else None
+            above = finish(tile, raw, exact)
+            if not exact:
+                highest = above if highest is None else jnp.maximum(highest, above)
+            raw = following
+        return highest
+
+    if first:
+        work(True)
+    else:
+        highest = jnp.max(work(False))
+
+        @pl.when(highest * SCALE > FAR)
+        def _():
+            work(True)
 
 
 def attend(flags, queries, bundles, layouts, states=None, own=None, sides=(0, 1), name="attend"):
@@ -212,12 +244,13 @@
 
 def merge_kernel(mine_ref, theirs_ref, out_ref):
     for head in range(GROUP):
-        top_a = mine_ref[head, HD + 8 : HD + 9, :]
-        top_b = theirs_ref[head, HD + 8 : HD + 9, :]
+        sum_a, sum_b = mine_ref[head, HD : HD + 1, :], theirs_ref[head, HD : HD + 1, :]
+        top_a = jnp.where(sum_a > 0.0, mine_ref[head, HD + 8 : HD + 9, :], MASKED)
+        top_b = jnp.where(sum_b > 0.0, theirs_ref[head, HD + 8 : HD + 9, :], MASKED)
         top = jnp.maximum(top_a, top_b)
         a = jnp.exp2((top_a - top) * SCALE)
         b = jnp.exp2((top_b - top) * SCALE)
-        total = mine_ref[head, HD : HD + 1, :] * a + theirs_ref[head, HD : HD + 1, :] * b
+        total = sum_a * a + sum_b * b
         summed = mine_ref[head, 0:HD, :] * a + theirs_ref[head, 0:HD, :] * b
         attended = jnp.transpose(summed / total, (1, 0))
         out_ref[:, head * HD : (head + 1) * HD] = attended.astype(jnp.bfloat16)

time: 160 us -> 159 us (level)
  the two profiles are of different devices: /device:TPU:2 before, /device:TPU:1 now
where the time goes in v3:
time: 159 us; the launch traced here: 156 us
  starting transfers between devices  69.4 us (44%)
  Pallas kernels  26.6 us (17%)
  waiting for transfers between devices  20.3 us (13%)
  blocking collectives  15.5 us (10%)
  between operations  14.1 us (9%)
  local copies, waits for them, and re-layouts  8.47 us (5%)
  other arithmetic  1.77 us (1%)
    pallas_call x6, Pallas kernels, attend(): pl.pallas_call(functools.partial(attend_kernel, layouts=layouts, sides=si...  20.2 us
    all_gather x1, blocking collectives, local(): line = lax.all_gather(unit, 'y', axis=0, tiled=False)  15.5 us
    ppermute x1, starting transfers between devices, local(): left = lax.ppermute(bundle, 'z', ring(8, 7))  13 us
    ppermute x3, starting transfers between devices, local(): gathered = [lax.ppermute(attended, 'x', ring(4, d)) for d in (1, 3, 2)]  12.3 us
    ppermute x1, starting transfers between devices, local(): back = lax.ppermute(left[512:], 'z', ring(8, 7))  8.95 us
    ppermute x1, starting transfers between devices, local(): other_queries = lax.ppermute(queries, 'c', swap)  8.78 us
    ppermute x1, waiting for transfers between devices, local(): crossing = lax.ppermute(far, 'h', swap)  8.54 us
    ppermute x2, starting transfers between devices, local(): next_left = lax.ppermute(left, 'z', ring(8, 7))  7.91 us
  transfers between devices with their start and end apart: 18, of which 6 were waited for; matrix products, arithmetic and copies ran while one was open for 2% of the time, Pallas kernels for 16%

profile of v3, /device:TPU:1, one launch (start us, length us, event | category | flops | bytes accessed | tf_op | source)
XLA Modules:
  0.0 156.1 jit_solution(13344938540581104688)
XLA Ops:
  6.5 8.8 %collective-permute-start.3 = (bf16[256,640]{1,0:T(8,128)(2,1)}, bf16[256,640]{1,0:T(8,128)(2,1)S(1)}, u32[]{:S(2)}, u32[]{:S(2)}) collective-permute-start(bf16[256,640]{1,0:T(8,128)(2,1)} %refs_1_.9), channel_id=1, source_target_pairs={{0,8},{8,0},{1,9},{9,1},{2,10},{10,2},{3,11},{11,3},{4,12},{12,4},... | collective-permute-start | bytes 983048 | tf_op jit(solution)/shard_map/ppermute | solution.py:337
  15.3 0.7 collective-permute-start.2
  16.0 1.3 collective-permute-start
  17.3 1.3 collective-permute-start.1
  18.6 0.8 broadcast_select_fusion.weight_ref
  19.5 1.2 collective-permute-done.1.far_vals
  20.7 0.8 copy-done.2
  21.5 0.8 copy-done.4
  22.3 0.7 copy-done.6
  23.0 0.4 pick.1
  23.5 15.5 %all-gather = bf16[2496,128]{1,0:T(8,128)(2,1)S(1)} all-gather(bf16[624,128]{1,0:T(8,128)(2,1)S(1)} %pick.1), channel_id=2, replica_groups=mesh['y'=4,'z'=8,'c'=2,'x'=4,'h'=2] {'y'}, dimensions={0}, use_global_device_ids=true | all-gather | bytes 798720 | tf_op jit(solution)/shard_map/all_gather | solution.py:341
  39.0 1.9 %collective-permute-start.4 = (bf16[1152,128]{1,0:T(8,128)(2,1)S(1)}, bf16[1152,128]{1,0:T(8,128)(2,1)S(1)}, u32[]{:S(2)}, u32[]{:S(2)}) collective-permute-start(bf16[1152,128]{1,0:T(8,128)(2,1)S(1)} %pad_maximum_fusion.refs_5_), channel_id=1, source_target_pairs={{0,16},{16,32},{32,48},{48,64},{64,80},{80,96},{96,112},{112,0},{1... | collective-permute-start | bytes 884744 | tf_op jit(solution)/shard_map/ppermute | solution.py:360
  40.9 13.0 %collective-permute-start.5 = (bf16[1152,128]{1,0:T(8,128)(2,1)S(1)}, bf16[1152,128]{1,0:T(8,128)(2,1)S(1)}, u32[]{:S(2)}, u32[]{:S(2)}) collective-permute-start(bf16[1152,128]{1,0:T(8,128)(2,1)S(1)} %pad_maximum_fusion.refs_5_), channel_id=1, source_target_pairs={{0,112},{16,0},{32,16},{48,32},{64,48},{80,64},{96,80},{112,96},{1... | collective-permute-start | bytes 884744 | tf_op jit(solution)/shard_map/ppermute | solution.py:361
  54.1 0.7 slice.22
  54.8 0.8 copy-done.3
  55.6 0.8 copy-done.5
  56.5 1.0 copy-done.7
  57.5 4.0 %attend0.1 = (f32[5,144,256]{2,1,0:T(8,128)S(1)}, f32[5,144,256]{2,1,0:T(8,128)S(1)}) custom-call(s32[10]{0:T(128)S(1)} %convert_element_type.23.refs_0_, bf16[256,640]{1,0:T(8,128)(2,1)S(1)} %copy-done.7, bf16[256,640]{1,0:T(8,128)(2,1)S(1)} %collective-permute-done.3.refs_2_.refs_1_, bf16[256,128]{1,0:T(8,128)(2,1)S(1)} %copy-done.3, ...), custom_call_target="tpu_custom_call" | custom-call | flops 2348810240 | bytes 4194304 | tf_op jit(solution)/shard_map/attend0/pallas_call | solution.py:221
  61.6 3.4 %collective-permute-start.9 = (bf16[1152,128]{1,0:T(8,128)(2,1)S(1)}, bf16[1152,128]{1,0:T(8,128)(2,1)S(1)}, u32[]{:S(2)}, u32[]{:S(2)}) collective-permute-start(bf16[1152,128]{1,0:T(8,128)(2,1)S(1)} %collective-permute-done.5.refs_4_), channel_id=1, source_target_pairs={{0,112},{16,0},{32,16},{48,32},{64,48},{80,64},{96,80},{112,96},{1... | collective-permute-start | bytes 884744 | tf_op jit(solution)/shard_map/ppermute | solution.py:368
  64.9 1.9 %collective-permute-start.6 = (bf16[1152,128]{1,0:T(8,128)(2,1)S(1)}, bf16[1152,128]{1,0:T(8,128)(2,1)S(1)}, u32[]{:S(2)}, u32[]{:S(2)}) collective-permute-start(bf16[1152,128]{1,0:T(8,128)(2,1)S(1)} %collective-permute-done.4.refs_3_), channel_id=1, source_target_pairs={{0,16},{16,32},{32,48},{48,64},{64,80},{80,96},{96,112},{112,0},{1... | collective-permute-start | bytes 884744 | tf_op jit(solution)/shard_map/ppermute | solution.py:367
  67.2 0.1 concatenate.24
  67.4 0.1 concatenate.23
  67.6 1.4 collective-permute-done.9.refs_4_
  69.0 4.6 %collective-permute-start.10 = (bf16[1152,128]{1,0:T(8,128)(2,1)S(1)}, bf16[1152,128]{1,0:T(8,128)(2,1)S(1)}, u32[]{:S(2)}, u32[]{:S(2)}) collective-permute-start(bf16[1152,128]{1,0:T(8,128)(2,1)S(1)} %collective-permute-done.9.refs_4_), channel_id=1, source_target_pairs={{0,112},{16,0},{32,16},{48,32},{64,48},{80,64},{96,80},{112,96},{1... | collective-permute-start | bytes 884744 | tf_op jit(solution)/shard_map/ppermute | solution.py:368
  73.6 1.9 %collective-permute-start.7 = (bf16[1152,128]{1,0:T(8,128)(2,1)S(1)}, bf16[1152,128]{1,0:T(8,128)(2,1)S(1)}, u32[]{:S(2)}, u32[]{:S(2)}) collective-permute-start(bf16[1152,128]{1,0:T(8,128)(2,1)S(1)} %collective-permute-done.6.refs_3_), channel_id=1, source_target_pairs={{0,16},{16,32},{32,48},{48,64},{64,80},{80,96},{96,112},{112,0},{1... | collective-permute-start | bytes 884744 | tf_op jit(solution)/shard_map/ppermute | solution.py:367
  75.5 4.3 %attend1.1 = (f32[5,144,256]{2,1,0:T(8,128)S(1)}, f32[5,144,256]{2,1,0:T(8,128)S(1)}) custom-call(s32[20]{0:T(128)S(1)} %convert_element_type.26.refs_0_, bf16[256,640]{1,0:T(8,128)(2,1)S(1)} %copy-done.8, bf16[256,640]{1,0:T(8,128)(2,1)S(1)} %collective-permute-done.3.refs_2_.refs_1_, bf16[1152,128]{1,0:T(8,128)(2,1)S(1)} %collective-permute-done.4.refs_3_, ...), custom_call_target="tpu_custom_call" | custom-call | flops 3019898880 | bytes 4194304 | tf_op jit(solution)/shard_map/attend1/pallas_call | solution.py:221
  79.8 4.1 %attend2.1 = (f32[5,144,256]{2,1,0:T(8,128)S(1)}, f32[5,144,256]{2,1,0:T(8,128)S(1)}) custom-call(s32[20]{0:T(128)S(1)} %convert_element_type.25.refs_0_, bf16[256,640]{1,0:T(8,128)(2,1)S(1)} %copy-done.8, bf16[256,640]{1,0:T(8,128)(2,1)S(1)} %collective-permute-done.3.refs_2_.refs_1_, bf16[1152,128]{1,0:T(8,128)(2,1)S(1)} %collective-permute-done.6.refs_3_, ...), custom_call_target="tpu_custom_call" | custom-call | flops 3019898880 | bytes 4194304 | tf_op jit(solution)/shard_map/attend2/pallas_call | solution.py:221
  84.0 8.9 %collective-permute-start.11 = (bf16[640,128]{1,0:T(8,128)(2,1)S(1)}, bf16[640,128]{1,0:T(8,128)(2,1)S(1)}, u32[]{:S(2)}, u32[]{:S(2)}) collective-permute-start(bf16[640,128]{1,0:T(8,128)(2,1)S(1)} %slice.24), channel_id=1, source_target_pairs={{0,112},{16,0},{32,16},{48,32},{64,48},{80,64},{96,80},{112,96},{1... | collective-permute-start | bytes 491528 | tf_op jit(solution)/shard_map/ppermute | solution.py:377
  92.9 2.1 %collective-permute-start.8 = (bf16[512,128]{1,0:T(8,128)(2,1)S(1)}, bf16[512,128]{1,0:T(8,128)(2,1)S(1)}, u32[]{:S(2)}, u32[]{:S(2)}) collective-permute-start(bf16[512,128]{1,0:T(8,128)(2,1)S(1)} %slice.23), channel_id=1, source_target_pairs={{0,16},{16,32},{32,48},{48,64},{64,80},{80,96},{96,112},{112,0},{1... | collective-permute-start | bytes 393224 | tf_op jit(solution)/shard_map/ppermute | solution.py:376
  95.1 4.1 %attend3.1 = (f32[5,144,256]{2,1,0:T(8,128)S(1)}, f32[5,144,256]{2,1,0:T(8,128)S(1)}) custom-call(s32[20]{0:T(128)S(1)} %convert_element_type.24.refs_0_, bf16[256,640]{1,0:T(8,128)(2,1)S(1)} %copy-done.8, bf16[256,640]{1,0:T(8,128)(2,1)S(1)} %collective-permute-done.3.refs_2_.refs_1_, bf16[1152,128]{1,0:T(8,128)(2,1)S(1)} %collective-permute-done.7.refs_3_, ...), custom_call_target="tpu_custom_call" | custom-call | flops 3019898880 | bytes 4194304 | tf_op jit(solution)/shard_map/attend3/pallas_call | solution.py:221
  99.2 2.4 %collective-permute-done.8.refs_2_ = bf16[512,128]{1,0:T(8,128)(2,1)S(1)} collective-permute-done((bf16[512,128]{1,0:T(8,128)(2,1)S(1)}, bf16[512,128]{1,0:T(8,128)(2,1)S(1)}, u32[]{:S(2)}, u32[]{:S(2)}) %collective-permute-start.8) | collective-permute-done | bytes 131104 | tf_op jit(solution)/shard_map/ppermute | solution.py:376
  101.6 1.9 %attend4b.1 = f32[5,144,256]{2,1,0:T(8,128)S(1)} custom-call(s32[20]{0:T(128)S(1)} %convert_element_type.22.refs_0_, bf16[256,640]{1,0:T(8,128)(2,1)S(1)} %collective-permute-done.3.refs_2_.refs_1_, bf16[512,128]{1,0:T(8,128)(2,1)S(1)} %collective-permute-done.8.refs_2_, bf16[640,128]{1,0:T(8,128)(2,1)S(1)} %collective-permute-done.11.refs_3_, ...), custom_call_target="tpu_custom_call" | custom-call | flops 838860800 | bytes 4194304 | tf_op jit(solution)/shard_map/attend4b/pallas_call | solution.py:221
  103.4 5.5 %collective-permute-start.12 = (f32[5,144,256]{2,1,0:T(8,128)S(1)}, f32[5,144,256]{2,1,0:T(8,128)S(1)}, u32[]{:S(2)}, u32[]{:S(2)}) collective-permute-start(f32[5,144,256]{2,1,0:T(8,128)S(1)} %attend4b.1), channel_id=1, source_target_pairs={{0,8},{8,0},{1,9},{9,1},{2,10},{10,2},{3,11},{11,3},{4,12},{12,4},... | collective-permute-start | bytes 2211848 | tf_op jit(solution)/shard_map/ppermute | solution.py:383
  108.9 1.9 %attend4a.1.mine_ref = f32[5,144,256]{2,1,0:T(8,128)S(1)} custom-call(s32[20]{0:T(128)S(1)} %convert_element_type.22.refs_0_, bf16[256,640]{1,0:T(8,128)(2,1)S(1)} %copy-done.8, bf16[512,128]{1,0:T(8,128)(2,1)S(1)} %collective-permute-done.8.refs_2_, bf16[640,128]{1,0:T(8,128)(2,1)S(1)} %collective-permute-done.11.refs_3_, ...), custom_call_target="tpu_custom_call" | custom-call | flops 838860800 | bytes 4194304 | tf_op jit(solution)/shard_map/attend4a/pallas_call | solution.py:221
  110.8 0.2 merge.1.refs_0_
  111.0 5.8 %collective-permute-start.13 = (bf16[256,640]{1,0:T(8,128)(2,1)S(1)}, bf16[256,640]{1,0:T(8,128)(2,1)S(1)}, u32[]{:S(2)}, u32[]{:S(2)}) collective-permute-start(bf16[256,640]{1,0:T(8,128)(2,1)S(1)} %merge.1.refs_0_), channel_id=1, source_target_pairs={{0,2},{2,4},{4,6},{6,0},{1,3},{3,5},{5,7},{7,1},{8,10},{10,12},{12... | collective-permute-start | bytes 983048 | tf_op jit(solution)/shard_map/ppermute | solution.py:390
  116.8 2.8 %collective-permute-start.14 = (bf16[256,640]{1,0:T(8,128)(2,1)S(1)}, bf16[256,640]{1,0:T(8,128)(2,1)S(1)}, u32[]{:S(2)}, u32[]{:S(2)}) collective-permute-start(bf16[256,640]{1,0:T(8,128)(2,1)S(1)} %merge.1.refs_0_), channel_id=1, source_target_pairs={{0,6},{2,0},{4,2},{6,4},{1,7},{3,1},{5,3},{7,5},{8,14},{10,8},{12,... | collective-permute-start | bytes 983048 | tf_op jit(solution)/shard_map/ppermute | solution.py:390
  119.6 3.7 %collective-permute-start.15 = (bf16[256,640]{1,0:T(8,128)(2,1)S(1)}, bf16[256,640]{1,0:T(8,128)(2,1)S(1)}, u32[]{:S(2)}, u32[]{:S(2)}) collective-permute-start(bf16[256,640]{1,0:T(8,128)(2,1)S(1)} %merge.1.refs_0_), channel_id=1, source_target_pairs={{0,4},{2,6},{4,0},{6,2},{1,5},{3,7},{5,1},{7,3},{8,12},{10,14},{12... | collective-permute-start | bytes 983048 | tf_op jit(solution)/shard_map/ppermute | solution.py:390
  123.5 2.1 %copy-done = bf16[64,240,128]{2,1,0:T(8,128)(2,1)S(1)} copy-done((bf16[64,240,128]{2,1,0:T(8,128)(2,1)S(1)}, bf16[64,240,128]{2,1,0:T(8,128)(2,1)}, u32[]{:S(2)}) %copy-start) | copy-done | bytes 3932184
  125.6 1.0 far0.1.refs_4_
  126.6 0.7 collective-permute-done.14.refs_1_
  127.3 6.0 %collective-permute-done.15.refs_2_ = bf16[256,640]{1,0:T(8,128)(2,1)S(1)} collective-permute-done((bf16[256,640]{1,0:T(8,128)(2,1)S(1)}, bf16[256,640]{1,0:T(8,128)(2,1)S(1)}, u32[]{:S(2)}, u32[]{:S(2)}) %collective-permute-start.15) | collective-permute-done | bytes 327712 | tf_op jit(solution)/shard_map/ppermute | solution.py:390
  133.3 1.9 %far1.1 = bf16[256,384]{1,0:T(8,128)(2,1)S(1)} custom-call(s32[4]{0:T(128)S(1)} %pad_add_fusion.at_ref, bf16[256,640]{1,0:T(8,128)(2,1)S(1)} %collective-permute-done.13.refs_0_, bf16[256,640]{1,0:T(8,128)(2,1)S(1)} %collective-permute-done.14.refs_1_, bf16[256,640]{1,0:T(8,128)(2,1)S(1)} %collective-permute-done.15.refs_2_, ...), custom_call_target="tpu_custom_call" | custom-call | flops 377487360 | bytes 1474560 | tf_op jit(solution)/shard_map/far1/pallas_call | solution.py:299
  135.2 1.9 %collective-permute-start.16 = (bf16[256,384]{1,0:T(8,128)(2,1)S(1)}, bf16[256,384]{1,0:T(8,128)(2,1)S(1)}, u32[]{:S(2)}, u32[]{:S(2)}) collective-permute-start(bf16[256,384]{1,0:T(8,128)(2,1)S(1)} %far1.1), channel_id=1, source_target_pairs={{0,1},{1,0},{2,3},{3,2},{4,5},{5,4},{6,7},{7,6},{8,9},{9,8},{10,11... | collective-permute-start | bytes 589832 | tf_op jit(solution)/shard_map/ppermute | solution.py:394
  137.1 1.0 near0.1.refs_4_
  138.1 1.9 %near1.1 = f32[256,384]{1,0:T(8,128)S(1)} custom-call(s32[4]{0:T(128)S(1)} %pad_add_fusion.at_ref, bf16[256,640]{1,0:T(8,128)(2,1)S(1)} %collective-permute-done.13.refs_0_, bf16[256,640]{1,0:T(8,128)(2,1)S(1)} %collective-permute-done.14.refs_1_, bf16[256,640]{1,0:T(8,128)(2,1)S(1)} %collective-permute-done.15.refs_2_, ...), custom_call_target="tpu_custom_call" | custom-call | flops 377487360 | bytes 1474560 | tf_op jit(solution)/shard_map/near1/pallas_call | solution.py:299
  140.0 8.5 %collective-permute-done.16 = bf16[256,384]{1,0:T(8,128)(2,1)S(1)} collective-permute-done((bf16[256,384]{1,0:T(8,128)(2,1)S(1)}, bf16[256,384]{1,0:T(8,128)(2,1)S(1)}, u32[]{:S(2)}, u32[]{:S(2)}) %collective-permute-start.16) | collective-permute-done | bytes 196640 | tf_op jit(solution)/shard_map/ppermute | solution.py:394
  148.5 0.7 add_convert_fusion
  (40 shorter events, 0.7 us)
Async XLA Ops:
  6.5 116.9 %all-gather.4.cloned.1.call-start = ((), (), s32[]{:S(2)}) async-start(), calls=%async_computation | async-start | bytes 4177920 | tf_op jit(solution)/shard_map/all_gather | solution.py:375
  6.5 16.9 %collective-permute-start.3 = (bf16[256,640]{1,0:T(8,128)(2,1)}, bf16[256,640]{1,0:T(8,128)(2,1)S(1)}, u32[]{:S(2)}, u32[]{:S(2)}) collective-permute-start(bf16[256,640]{1,0:T(8,128)(2,1)} %refs_1_.9), channel_id=1, source_target_pairs={{0,8},{8,0},{1,9},{9,1},{2,10},{10,2},{3,11},{11,3},{4,12},{12,4},... | collective-permute-start | bytes 983048 | tf_op jit(solution)/shard_map/ppermute | solution.py:337
  15.3 3.3 %collective-permute-start.2 = (bf16[80,384]{1,0:T(8,128)(2,1)}, bf16[80,384]{1,0:T(8,128)(2,1)S(1)}, u32[]{:S(2)}, u32[]{:S(2)}) collective-permute-start(bf16[80,384]{1,0:T(8,128)(2,1)} %param.9), channel_id=1, source_target_pairs={{1,448},{17,464},{33,480},{49,496},{64,385},{80,401},{96,417},{112... | collective-permute-start | bytes 184328 | tf_op jit(solution)/shard_map/ppermute | solution.py:335
  16.0 3.5 %collective-permute-start = (bf16[256,128]{1,0:T(8,128)(2,1)}, bf16[256,128]{1,0:T(8,128)(2,1)S(1)}, u32[]{:S(2)}, u32[]{:S(2)}) collective-permute-start(bf16[256,128]{1,0:T(8,128)(2,1)} %refs_3_.1), channel_id=1, source_target_pairs={{0,8},{1,9},{2,10},{3,11},{4,12},{5,13},{6,14},{7,15}} | collective-permute-start | bytes 196616 | tf_op jit(solution)/shard_map/ppermute | solution.py:328
  17.3 3.4 %collective-permute-start.1 = (bf16[256,128]{1,0:T(8,128)(2,1)}, bf16[256,128]{1,0:T(8,128)(2,1)S(1)}, u32[]{:S(2)}, u32[]{:S(2)}) collective-permute-start(bf16[256,128]{1,0:T(8,128)(2,1)} %refs_4_.1), channel_id=1, source_target_pairs={{0,8},{1,9},{2,10},{3,11},{4,12},{5,13},{6,14},{7,15}} | collective-permute-start | bytes 196616 | tf_op jit(solution)/shard_map/ppermute | solution.py:328
  20.7 0.8 copy-start.2
  21.5 0.8 copy-start.4
  22.3 0.7 copy-start.6
  39.0 22.5 %collective-permute-start.4 = (bf16[1152,128]{1,0:T(8,128)(2,1)S(1)}, bf16[1152,128]{1,0:T(8,128)(2,1)S(1)}, u32[]{:S(2)}, u32[]{:S(2)}) collective-permute-start(bf16[1152,128]{1,0:T(8,128)(2,1)S(1)} %pad_maximum_fusion.refs_5_), channel_id=1, source_target_pairs={{0,16},{16,32},{32,48},{48,64},{64,80},{80,96},{96,112},{112,0},{1... | collective-permute-start | bytes 884744 | tf_op jit(solution)/shard_map/ppermute | solution.py:360
  40.9 20.6 %collective-permute-start.5 = (bf16[1152,128]{1,0:T(8,128)(2,1)S(1)}, bf16[1152,128]{1,0:T(8,128)(2,1)S(1)}, u32[]{:S(2)}, u32[]{:S(2)}) collective-permute-start(bf16[1152,128]{1,0:T(8,128)(2,1)S(1)} %pad_maximum_fusion.refs_5_), channel_id=1, source_target_pairs={{0,112},{16,0},{32,16},{48,32},{64,48},{80,64},{96,80},{112,96},{1... | collective-permute-start | bytes 884744 | tf_op jit(solution)/shard_map/ppermute | solution.py:361
  54.8 0.8 copy-start.3
  55.6 0.8 copy-start.5
  56.5 1.0 copy-start.7
  57.5 18.1 %copy-start.8 = (bf16[256,640]{1,0:T(8,128)(2,1)S(1)}, bf16[256,640]{1,0:T(8,128)(2,1)}, u32[]{:S(2)}) copy-start(bf16[256,640]{1,0:T(8,128)(2,1)} %refs_1_.9) | copy-start | bytes 983044
  61.6 7.5 %collective-permute-start.9 = (bf16[1152,128]{1,0:T(8,128)(2,1)S(1)}, bf16[1152,128]{1,0:T(8,128)(2,1)S(1)}, u32[]{:S(2)}, u32[]{:S(2)}) collective-permute-start(bf16[1152,128]{1,0:T(8,128)(2,1)S(1)} %collective-permute-done.5.refs_4_), channel_id=1, source_target_pairs={{0,112},{16,0},{32,16},{48,32},{64,48},{80,64},{96,80},{112,96},{1... | collective-permute-start | bytes 884744 | tf_op jit(solution)/shard_map/ppermute | solution.py:368
  64.9 8.7 %collective-permute-start.6 = (bf16[1152,128]{1,0:T(8,128)(2,1)S(1)}, bf16[1152,128]{1,0:T(8,128)(2,1)S(1)}, u32[]{:S(2)}, u32[]{:S(2)}) collective-permute-start(bf16[1152,128]{1,0:T(8,128)(2,1)S(1)} %collective-permute-done.4.refs_3_), channel_id=1, source_target_pairs={{0,16},{16,32},{32,48},{48,64},{64,80},{80,96},{96,112},{112,0},{1... | collective-permute-start | bytes 884744 | tf_op jit(solution)/shard_map/ppermute | solution.py:367
  69.0 14.9 %collective-permute-start.10 = (bf16[1152,128]{1,0:T(8,128)(2,1)S(1)}, bf16[1152,128]{1,0:T(8,128)(2,1)S(1)}, u32[]{:S(2)}, u32[]{:S(2)}) collective-permute-start(bf16[1152,128]{1,0:T(8,128)(2,1)S(1)} %collective-permute-done.9.refs_4_), channel_id=1, source_target_pairs={{0,112},{16,0},{32,16},{48,32},{64,48},{80,64},{96,80},{112,96},{1... | collective-permute-start | bytes 884744 | tf_op jit(solution)/shard_map/ppermute | solution.py:368
  73.6 19.3 %collective-permute-start.7 = (bf16[1152,128]{1,0:T(8,128)(2,1)S(1)}, bf16[1152,128]{1,0:T(8,128)(2,1)S(1)}, u32[]{:S(2)}, u32[]{:S(2)}) collective-permute-start(bf16[1152,128]{1,0:T(8,128)(2,1)S(1)} %collective-permute-done.6.refs_3_), channel_id=1, source_target_pairs={{0,16},{16,32},{32,48},{48,64},{64,80},{80,96},{96,112},{112,0},{1... | collective-permute-start | bytes 884744 | tf_op jit(solution)/shard_map/ppermute | solution.py:367
  84.0 17.6 %collective-permute-start.11 = (bf16[640,128]{1,0:T(8,128)(2,1)S(1)}, bf16[640,128]{1,0:T(8,128)(2,1)S(1)}, u32[]{:S(2)}, u32[]{:S(2)}) collective-permute-start(bf16[640,128]{1,0:T(8,128)(2,1)S(1)} %slice.24), channel_id=1, source_target_pairs={{0,112},{16,0},{32,16},{48,32},{64,48},{80,64},{96,80},{112,96},{1... | collective-permute-start | bytes 491528 | tf_op jit(solution)/shard_map/ppermute | solution.py:377
  92.9 8.6 %collective-permute-start.8 = (bf16[512,128]{1,0:T(8,128)(2,1)S(1)}, bf16[512,128]{1,0:T(8,128)(2,1)S(1)}, u32[]{:S(2)}, u32[]{:S(2)}) collective-permute-start(bf16[512,128]{1,0:T(8,128)(2,1)S(1)} %slice.23), channel_id=1, source_target_pairs={{0,16},{16,32},{32,48},{48,64},{64,80},{80,96},{96,112},{112,0},{1... | collective-permute-start | bytes 393224 | tf_op jit(solution)/shard_map/ppermute | solution.py:376
  103.4 7.3 %collective-permute-start.12 = (f32[5,144,256]{2,1,0:T(8,128)S(1)}, f32[5,144,256]{2,1,0:T(8,128)S(1)}, u32[]{:S(2)}, u32[]{:S(2)}) collective-permute-start(f32[5,144,256]{2,1,0:T(8,128)S(1)} %attend4b.1), channel_id=1, source_target_pairs={{0,8},{8,0},{1,9},{9,1},{2,10},{10,2},{3,11},{11,3},{4,12},{12,4},... | collective-permute-start | bytes 2211848 | tf_op jit(solution)/shard_map/ppermute | solution.py:383
  111.0 15.6 %collective-permute-start.13 = (bf16[256,640]{1,0:T(8,128)(2,1)S(1)}, bf16[256,640]{1,0:T(8,128)(2,1)S(1)}, u32[]{:S(2)}, u32[]{:S(2)}) collective-permute-start(bf16[256,640]{1,0:T(8,128)(2,1)S(1)} %merge.1.refs_0_), channel_id=1, source_target_pairs={{0,2},{2,4},{4,6},{6,0},{1,3},{3,5},{5,7},{7,1},{8,10},{10,12},{12... | collective-permute-start | bytes 983048 | tf_op jit(solution)/shard_map/ppermute | solution.py:390
  116.8 10.6 %collective-permute-start.14 = (bf16[256,640]{1,0:T(8,128)(2,1)S(1)}, bf16[256,640]{1,0:T(8,128)(2,1)S(1)}, u32[]{:S(2)}, u32[]{:S(2)}) collective-permute-start(bf16[256,640]{1,0:T(8,128)(2,1)S(1)} %merge.1.refs_0_), channel_id=1, source_target_pairs={{0,6},{2,0},{4,2},{6,4},{1,7},{3,1},{5,3},{7,5},{8,14},{10,8},{12,... | collective-permute-start | bytes 983048 | tf_op jit(solution)/shard_map/ppermute | solution.py:390
  119.6 13.8 %collective-permute-start.15 = (bf16[256,640]{1,0:T(8,128)(2,1)S(1)}, bf16[256,640]{1,0:T(8,128)(2,1)S(1)}, u32[]{:S(2)}, u32[]{:S(2)}) collective-permute-start(bf16[256,640]{1,0:T(8,128)(2,1)S(1)} %merge.1.refs_0_), channel_id=1, source_target_pairs={{0,4},{2,6},{4,0},{6,2},{1,5},{3,7},{5,1},{7,3},{8,12},{10,14},{12... | collective-permute-start | bytes 983048 | tf_op jit(solution)/shard_map/ppermute | solution.py:390
  123.5 2.1 %copy-start = (bf16[64,240,128]{2,1,0:T(8,128)(2,1)S(1)}, bf16[64,240,128]{2,1,0:T(8,128)(2,1)}, u32[]{:S(2)}) copy-start(bf16[64,240,128]{2,1,0:T(8,128)(2,1)} %all-gather.4.cloned.1.call-done) | copy-start | bytes 11796484
  125.6 7.7 %copy-start.1 = (bf16[64,240,128]{2,1,0:T(8,128)(2,1)S(1)}, bf16[64,240,128]{2,1,0:T(8,128)(2,1)}, u32[]{:S(2)}) copy-start(bf16[64,240,128]{2,1,0:T(8,128)(2,1)} %all-gather.4.cloned.1.call-done) | copy-start | bytes 11796484
  135.2 13.3 %collective-permute-start.16 = (bf16[256,384]{1,0:T(8,128)(2,1)S(1)}, bf16[256,384]{1,0:T(8,128)(2,1)S(1)}, u32[]{:S(2)}, u32[]{:S(2)}) collective-permute-start(bf16[256,384]{1,0:T(8,128)(2,1)S(1)} %far1.1), channel_id=1, source_target_pairs={{0,1},{1,0},{2,3},{3,2},{4,5},{5,4},{6,7},{7,6},{8,9},{9,8},{10,11... | collective-permute-start | bytes 589832 | tf_op jit(solution)/shard_map/ppermute | solution.py:394
Sparse Core Ops, SparseCore 0:
  61.7 48.1 all-gather.3

commit v4 on v3

--- a/solution.py
+++ b/solution.py
@@ -386,8 +386,8 @@
 
     weight = weight.reshape(2, 8, 4, 3, out_weight.shape[0], HD)
     nearby = jnp.stack([x, h]).astype(jnp.int32)
-    across = jnp.stack([(x + 3) % 4, (x + 1) % 4, (x + 2) % 4, h]).astype(jnp.int32)
-    gathered = [lax.ppermute(attended, "x", ring(4, d)) for d in (1, 3, 2)]
+    across = jnp.stack([(x + 2) % 4, (x + 3) % 4, (x + 1) % 4, h]).astype(jnp.int32)
+    gathered = [lax.ppermute(attended, "x", ring(4, d)) for d in (2, 1, 3)]
     far = project(nearby, [attended], weight, "far", name="far0")
     near = project(nearby, [attended], weight, "near", name="near0")
     far = project(across, gathered, weight, "far", far, jnp.bfloat16, name="far1")

time: 159 us -> 159 us (level)
  transfers between devices with their start and end apart: 18 -> 18, of which waited for: 6 -> 5; matrix products, arithmetic and copies ran while one was open for 2% -> 2% of each run, Pallas kernels for 16% -> 16%
where the time goes in v4:
time: 159 us; the launch traced here: 156 us
  starting transfers between devices  70.9 us (45%)
  Pallas kernels  26.6 us (17%)
  waiting for transfers between devices  19 us (12%)
  blocking collectives  15.5 us (10%)
  between operations  14.1 us (9%)
  local copies, waits for them, and re-layouts  8.47 us (5%)
  other arithmetic  1.77 us (1%)
    pallas_call x6, Pallas kernels, attend(): pl.pallas_call(functools.partial(attend_kernel, layouts=layouts, sides=si...  20.2 us
    all_gather x1, blocking collectives, local(): line = lax.all_gather(unit, 'y', axis=0, tiled=False)  15.5 us
    ppermute x3, starting transfers between devices, local(): gathered = [lax.ppermute(attended, 'x', ring(4, d)) for d in (2, 1, 3)]  13.8 us
    ppermute x1, starting transfers between devices, local(): left = lax.ppermute(bundle, 'z', ring(8, 7))  13 us
    ppermute x1, starting transfers between devices, local(): back = lax.ppermute(left[512:], 'z', ring(8, 7))  8.95 us
    ppermute x1, starting transfers between devices, local(): other_queries = lax.ppermute(queries, 'c', swap)  8.78 us
    ppermute x1, waiting for transfers between devices, local(): crossing = lax.ppermute(far, 'h', swap)  8.62 us
    ppermute x2, starting transfers between devices, local(): next_left = lax.ppermute(left, 'z', ring(8, 7))  7.91 us
  transfers between devices with their start and end apart: 18, of which 5 were waited for; matrix products, arithmetic and copies ran while one was open for 2% of the time, Pallas kernels for 16%

profile of v4, /device:TPU:1, one launch (start us, length us, event | category | flops | bytes accessed | tf_op | source)
XLA Modules:
  0.0 156.3 jit_solution(2508750336478397718)
XLA Ops:
  6.5 8.8 %collective-permute-start.3 = (bf16[256,640]{1,0:T(8,128)(2,1)}, bf16[256,640]{1,0:T(8,128)(2,1)S(1)}, u32[]{:S(2)}, u32[]{:S(2)}) collective-permute-start(bf16[256,640]{1,0:T(8,128)(2,1)} %refs_1_.9), channel_id=1, source_target_pairs={{0,8},{8,0},{1,9},{9,1},{2,10},{10,2},{3,11},{11,3},{4,12},{12,4},... | collective-permute-start | bytes 983048 | tf_op jit(solution)/shard_map/ppermute | solution.py:337
  15.3 0.7 collective-permute-start.2
  16.0 1.3 collective-permute-start
  17.3 1.3 collective-permute-start.1
  18.6 0.8 broadcast_select_fusion.weight_ref
  19.5 1.2 collective-permute-done.1.far_vals
  20.7 0.8 copy-done.2
  21.5 0.8 copy-done.4
  22.3 0.7 copy-done.6
  23.0 0.4 pick.1
  23.5 15.5 %all-gather = bf16[2496,128]{1,0:T(8,128)(2,1)S(1)} all-gather(bf16[624,128]{1,0:T(8,128)(2,1)S(1)} %pick.1), channel_id=2, replica_groups=mesh['y'=4,'z'=8,'c'=2,'x'=4,'h'=2] {'y'}, dimensions={0}, use_global_device_ids=true | all-gather | bytes 798720 | tf_op jit(solution)/shard_map/all_gather | solution.py:341
  39.0 1.9 %collective-permute-start.4 = (bf16[1152,128]{1,0:T(8,128)(2,1)S(1)}, bf16[1152,128]{1,0:T(8,128)(2,1)S(1)}, u32[]{:S(2)}, u32[]{:S(2)}) collective-permute-start(bf16[1152,128]{1,0:T(8,128)(2,1)S(1)} %pad_maximum_fusion.refs_5_), channel_id=1, source_target_pairs={{0,16},{16,32},{32,48},{48,64},{64,80},{80,96},{96,112},{112,0},{1... | collective-permute-start | bytes 884744 | tf_op jit(solution)/shard_map/ppermute | solution.py:360
  40.9 13.0 %collective-permute-start.5 = (bf16[1152,128]{1,0:T(8,128)(2,1)S(1)}, bf16[1152,128]{1,0:T(8,128)(2,1)S(1)}, u32[]{:S(2)}, u32[]{:S(2)}) collective-permute-start(bf16[1152,128]{1,0:T(8,128)(2,1)S(1)} %pad_maximum_fusion.refs_5_), channel_id=1, source_target_pairs={{0,112},{16,0},{32,16},{48,32},{64,48},{80,64},{96,80},{112,96},{1... | collective-permute-start | bytes 884744 | tf_op jit(solution)/shard_map/ppermute | solution.py:361
  54.1 0.7 slice.22
  54.8 0.8 copy-done.3
  55.6 0.8 copy-done.5
  56.5 1.0 copy-done.7
  57.5 4.0 %attend0.1 = (f32[5,144,256]{2,1,0:T(8,128)S(1)}, f32[5,144,256]{2,1,0:T(8,128)S(1)}) custom-call(s32[10]{0:T(128)S(1)} %convert_element_type.23.refs_0_, bf16[256,640]{1,0:T(8,128)(2,1)S(1)} %copy-done.7, bf16[256,640]{1,0:T(8,128)(2,1)S(1)} %collective-permute-done.3.refs_2_.refs_1_, bf16[256,128]{1,0:T(8,128)(2,1)S(1)} %copy-done.3, ...), custom_call_target="tpu_custom_call" | custom-call | flops 2348810240 | bytes 4194304 | tf_op jit(solution)/shard_map/attend0/pallas_call | solution.py:221
  61.6 3.4 %collective-permute-start.9 = (bf16[1152,128]{1,0:T(8,128)(2,1)S(1)}, bf16[1152,128]{1,0:T(8,128)(2,1)S(1)}, u32[]{:S(2)}, u32[]{:S(2)}) collective-permute-start(bf16[1152,128]{1,0:T(8,128)(2,1)S(1)} %collective-permute-done.5.refs_4_), channel_id=1, source_target_pairs={{0,112},{16,0},{32,16},{48,32},{64,48},{80,64},{96,80},{112,96},{1... | collective-permute-start | bytes 884744 | tf_op jit(solution)/shard_map/ppermute | solution.py:368
  64.9 1.9 %collective-permute-start.6 = (bf16[1152,128]{1,0:T(8,128)(2,1)S(1)}, bf16[1152,128]{1,0:T(8,128)(2,1)S(1)}, u32[]{:S(2)}, u32[]{:S(2)}) collective-permute-start(bf16[1152,128]{1,0:T(8,128)(2,1)S(1)} %collective-permute-done.4.refs_3_), channel_id=1, source_target_pairs={{0,16},{16,32},{32,48},{48,64},{64,80},{80,96},{96,112},{112,0},{1... | collective-permute-start | bytes 884744 | tf_op jit(solution)/shard_map/ppermute | solution.py:367
  67.0 0.1 concatenate.25
  67.2 0.1 concatenate.24
  67.4 0.1 concatenate.23
  67.6 1.4 collective-permute-done.9.refs_4_
  69.0 4.6 %collective-permute-start.10 = (bf16[1152,128]{1,0:T(8,128)(2,1)S(1)}, bf16[1152,128]{1,0:T(8,128)(2,1)S(1)}, u32[]{:S(2)}, u32[]{:S(2)}) collective-permute-start(bf16[1152,128]{1,0:T(8,128)(2,1)S(1)} %collective-permute-done.9.refs_4_), channel_id=1, source_target_pairs={{0,112},{16,0},{32,16},{48,32},{64,48},{80,64},{96,80},{112,96},{1... | collective-permute-start | bytes 884744 | tf_op jit(solution)/shard_map/ppermute | solution.py:368
  73.6 1.9 %collective-permute-start.7 = (bf16[1152,128]{1,0:T(8,128)(2,1)S(1)}, bf16[1152,128]{1,0:T(8,128)(2,1)S(1)}, u32[]{:S(2)}, u32[]{:S(2)}) collective-permute-start(bf16[1152,128]{1,0:T(8,128)(2,1)S(1)} %collective-permute-done.6.refs_3_), channel_id=1, source_target_pairs={{0,16},{16,32},{32,48},{48,64},{64,80},{80,96},{96,112},{112,0},{1... | collective-permute-start | bytes 884744 | tf_op jit(solution)/shard_map/ppermute | solution.py:367
  75.5 4.3 %attend1.1 = (f32[5,144,256]{2,1,0:T(8,128)S(1)}, f32[5,144,256]{2,1,0:T(8,128)S(1)}) custom-call(s32[20]{0:T(128)S(1)} %convert_element_type.26.refs_0_, bf16[256,640]{1,0:T(8,128)(2,1)S(1)} %copy-done.8, bf16[256,640]{1,0:T(8,128)(2,1)S(1)} %collective-permute-done.3.refs_2_.refs_1_, bf16[1152,128]{1,0:T(8,128)(2,1)S(1)} %collective-permute-done.4.refs_3_, ...), custom_call_target="tpu_custom_call" | custom-call | flops 3019898880 | bytes 4194304 | tf_op jit(solution)/shard_map/attend1/pallas_call | solution.py:221
  79.8 4.1 %attend2.1 = (f32[5,144,256]{2,1,0:T(8,128)S(1)}, f32[5,144,256]{2,1,0:T(8,128)S(1)}) custom-call(s32[20]{0:T(128)S(1)} %convert_element_type.25.refs_0_, bf16[256,640]{1,0:T(8,128)(2,1)S(1)} %copy-done.8, bf16[256,640]{1,0:T(8,128)(2,1)S(1)} %collective-permute-done.3.refs_2_.refs_1_, bf16[1152,128]{1,0:T(8,128)(2,1)S(1)} %collective-permute-done.6.refs_3_, ...), custom_call_target="tpu_custom_call" | custom-call | flops 3019898880 | bytes 4194304 | tf_op jit(solution)/shard_map/attend2/pallas_call | solution.py:221
  84.0 8.9 %collective-permute-start.11 = (bf16[640,128]{1,0:T(8,128)(2,1)S(1)}, bf16[640,128]{1,0:T(8,128)(2,1)S(1)}, u32[]{:S(2)}, u32[]{:S(2)}) collective-permute-start(bf16[640,128]{1,0:T(8,128)(2,1)S(1)} %slice.24), channel_id=1, source_target_pairs={{0,112},{16,0},{32,16},{48,32},{64,48},{80,64},{96,80},{112,96},{1... | collective-permute-start | bytes 491528 | tf_op jit(solution)/shard_map/ppermute | solution.py:377
  92.9 2.1 %collective-permute-start.8 = (bf16[512,128]{1,0:T(8,128)(2,1)S(1)}, bf16[512,128]{1,0:T(8,128)(2,1)S(1)}, u32[]{:S(2)}, u32[]{:S(2)}) collective-permute-start(bf16[512,128]{1,0:T(8,128)(2,1)S(1)} %slice.23), channel_id=1, source_target_pairs={{0,16},{16,32},{32,48},{48,64},{64,80},{80,96},{96,112},{112,0},{1... | collective-permute-start | bytes 393224 | tf_op jit(solution)/shard_map/ppermute | solution.py:376
  95.1 4.1 %attend3.1 = (f32[5,144,256]{2,1,0:T(8,128)S(1)}, f32[5,144,256]{2,1,0:T(8,128)S(1)}) custom-call(s32[20]{0:T(128)S(1)} %convert_element_type.24.refs_0_, bf16[256,640]{1,0:T(8,128)(2,1)S(1)} %copy-done.8, bf16[256,640]{1,0:T(8,128)(2,1)S(1)} %collective-permute-done.3.refs_2_.refs_1_, bf16[1152,128]{1,0:T(8,128)(2,1)S(1)} %collective-permute-done.7.refs_3_, ...), custom_call_target="tpu_custom_call" | custom-call | flops 3019898880 | bytes 4194304 | tf_op jit(solution)/shard_map/attend3/pallas_call | solution.py:221
  99.2 2.4 %collective-permute-done.8.refs_2_ = bf16[512,128]{1,0:T(8,128)(2,1)S(1)} collective-permute-done((bf16[512,128]{1,0:T(8,128)(2,1)S(1)}, bf16[512,128]{1,0:T(8,128)(2,1)S(1)}, u32[]{:S(2)}, u32[]{:S(2)}) %collective-permute-start.8) | collective-permute-done | bytes 131104 | tf_op jit(solution)/shard_map/ppermute | solution.py:376
  101.6 1.9 %attend4b.1 = f32[5,144,256]{2,1,0:T(8,128)S(1)} custom-call(s32[20]{0:T(128)S(1)} %convert_element_type.22.refs_0_, bf16[256,640]{1,0:T(8,128)(2,1)S(1)} %collective-permute-done.3.refs_2_.refs_1_, bf16[512,128]{1,0:T(8,128)(2,1)S(1)} %collective-permute-done.8.refs_2_, bf16[640,128]{1,0:T(8,128)(2,1)S(1)} %collective-permute-done.11.refs_3_, ...), custom_call_target="tpu_custom_call" | custom-call | flops 838860800 | bytes 4194304 | tf_op jit(solution)/shard_map/attend4b/pallas_call | solution.py:221
  103.4 5.5 %collective-permute-start.12 = (f32[5,144,256]{2,1,0:T(8,128)S(1)}, f32[5,144,256]{2,1,0:T(8,128)S(1)}, u32[]{:S(2)}, u32[]{:S(2)}) collective-permute-start(f32[5,144,256]{2,1,0:T(8,128)S(1)} %attend4b.1), channel_id=1, source_target_pairs={{0,8},{8,0},{1,9},{9,1},{2,10},{10,2},{3,11},{11,3},{4,12},{12,4},... | collective-permute-start | bytes 2211848 | tf_op jit(solution)/shard_map/ppermute | solution.py:383
  108.9 1.9 %attend4a.1.mine_ref = f32[5,144,256]{2,1,0:T(8,128)S(1)} custom-call(s32[20]{0:T(128)S(1)} %convert_element_type.22.refs_0_, bf16[256,640]{1,0:T(8,128)(2,1)S(1)} %copy-done.8, bf16[512,128]{1,0:T(8,128)(2,1)S(1)} %collective-permute-done.8.refs_2_, bf16[640,128]{1,0:T(8,128)(2,1)S(1)} %collective-permute-done.11.refs_3_, ...), custom_call_target="tpu_custom_call" | custom-call | flops 838860800 | bytes 4194304 | tf_op jit(solution)/shard_map/attend4a/pallas_call | solution.py:221
  110.8 0.2 merge.1.refs_0_
  111.0 7.3 %collective-permute-start.13 = (bf16[256,640]{1,0:T(8,128)(2,1)S(1)}, bf16[256,640]{1,0:T(8,128)(2,1)S(1)}, u32[]{:S(2)}, u32[]{:S(2)}) collective-permute-start(bf16[256,640]{1,0:T(8,128)(2,1)S(1)} %merge.1.refs_0_), channel_id=1, source_target_pairs={{0,4},{2,6},{4,0},{6,2},{1,5},{3,7},{5,1},{7,3},{8,12},{10,14},{12... | collective-permute-start | bytes 983048 | tf_op jit(solution)/shard_map/ppermute | solution.py:390
  118.3 2.2 %collective-permute-start.14 = (bf16[256,640]{1,0:T(8,128)(2,1)S(1)}, bf16[256,640]{1,0:T(8,128)(2,1)S(1)}, u32[]{:S(2)}, u32[]{:S(2)}) collective-permute-start(bf16[256,640]{1,0:T(8,128)(2,1)S(1)} %merge.1.refs_0_), channel_id=1, source_target_pairs={{0,2},{2,4},{4,6},{6,0},{1,3},{3,5},{5,7},{7,1},{8,10},{10,12},{12... | collective-permute-start | bytes 983048 | tf_op jit(solution)/shard_map/ppermute | solution.py:390
  120.5 4.3 %collective-permute-start.15 = (bf16[256,640]{1,0:T(8,128)(2,1)S(1)}, bf16[256,640]{1,0:T(8,128)(2,1)S(1)}, u32[]{:S(2)}, u32[]{:S(2)}) collective-permute-start(bf16[256,640]{1,0:T(8,128)(2,1)S(1)} %merge.1.refs_0_), channel_id=1, source_target_pairs={{0,6},{2,0},{4,2},{6,4},{1,7},{3,1},{5,3},{7,5},{8,14},{10,8},{12,... | collective-permute-start | bytes 983048 | tf_op jit(solution)/shard_map/ppermute | solution.py:390
  125.0 2.1 %copy-done = bf16[64,240,128]{2,1,0:T(8,128)(2,1)S(1)} copy-done((bf16[64,240,128]{2,1,0:T(8,128)(2,1)S(1)}, bf16[64,240,128]{2,1,0:T(8,128)(2,1)}, u32[]{:S(2)}) %copy-start) | copy-done | bytes 3932184
  127.1 1.0 far0.1.refs_4_
  128.1 5.3 %collective-permute-done.14.refs_1_ = bf16[256,640]{1,0:T(8,128)(2,1)S(1)} collective-permute-done((bf16[256,640]{1,0:T(8,128)(2,1)S(1)}, bf16[256,640]{1,0:T(8,128)(2,1)S(1)}, u32[]{:S(2)}, u32[]{:S(2)}) %collective-permute-start.14) | collective-permute-done | bytes 327712 | tf_op jit(solution)/shard_map/ppermute | solution.py:390
  133.5 1.9 %far1.1 = bf16[256,384]{1,0:T(8,128)(2,1)S(1)} custom-call(s32[4]{0:T(128)S(1)} %pad_add_fusion.at_ref, bf16[256,640]{1,0:T(8,128)(2,1)S(1)} %collective-permute-done.13.refs_0_, bf16[256,640]{1,0:T(8,128)(2,1)S(1)} %collective-permute-done.14.refs_1_, bf16[256,640]{1,0:T(8,128)(2,1)S(1)} %collective-permute-done.15.refs_2_, ...), custom_call_target="tpu_custom_call" | custom-call | flops 377487360 | bytes 1474560 | tf_op jit(solution)/shard_map/far1/pallas_call | solution.py:299
  135.3 1.9 %collective-permute-start.16 = (bf16[256,384]{1,0:T(8,128)(2,1)S(1)}, bf16[256,384]{1,0:T(8,128)(2,1)S(1)}, u32[]{:S(2)}, u32[]{:S(2)}) collective-permute-start(bf16[256,384]{1,0:T(8,128)(2,1)S(1)} %far1.1), channel_id=1, source_target_pairs={{0,1},{1,0},{2,3},{3,2},{4,5},{5,4},{6,7},{7,6},{8,9},{9,8},{10,11... | collective-permute-start | bytes 589832 | tf_op jit(solution)/shard_map/ppermute | solution.py:394
  137.3 1.0 near0.1.refs_4_
  138.3 1.9 %near1.1 = f32[256,384]{1,0:T(8,128)S(1)} custom-call(s32[4]{0:T(128)S(1)} %pad_add_fusion.at_ref, bf16[256,640]{1,0:T(8,128)(2,1)S(1)} %collective-permute-done.13.refs_0_, bf16[256,640]{1,0:T(8,128)(2,1)S(1)} %collective-permute-done.14.refs_1_, bf16[256,640]{1,0:T(8,128)(2,1)S(1)} %collective-permute-done.15.refs_2_, ...), custom_call_target="tpu_custom_call" | custom-call | flops 377487360 | bytes 1474560 | tf_op jit(solution)/shard_map/near1/pallas_call | solution.py:299
  140.2 8.6 %collective-permute-done.16 = bf16[256,384]{1,0:T(8,128)(2,1)S(1)} collective-permute-done((bf16[256,384]{1,0:T(8,128)(2,1)S(1)}, bf16[256,384]{1,0:T(8,128)(2,1)S(1)}, u32[]{:S(2)}, u32[]{:S(2)}) %collective-permute-start.16) | collective-permute-done | bytes 196640 | tf_op jit(solution)/shard_map/ppermute | solution.py:394
  148.8 0.7 add_convert_fusion
  (40 shorter events, 0.6 us)
Async XLA Ops:
  6.5 118.5 %all-gather.4.cloned.1.call-start = ((), (), s32[]{:S(2)}) async-start(), calls=%async_computation | async-start | bytes 4177920 | tf_op jit(solution)/shard_map/all_gather | solution.py:375
  6.5 16.9 %collective-permute-start.3 = (bf16[256,640]{1,0:T(8,128)(2,1)}, bf16[256,640]{1,0:T(8,128)(2,1)S(1)}, u32[]{:S(2)}, u32[]{:S(2)}) collective-permute-start(bf16[256,640]{1,0:T(8,128)(2,1)} %refs_1_.9), channel_id=1, source_target_pairs={{0,8},{8,0},{1,9},{9,1},{2,10},{10,2},{3,11},{11,3},{4,12},{12,4},... | collective-permute-start | bytes 983048 | tf_op jit(solution)/shard_map/ppermute | solution.py:337
  15.3 3.3 %collective-permute-start.2 = (bf16[80,384]{1,0:T(8,128)(2,1)}, bf16[80,384]{1,0:T(8,128)(2,1)S(1)}, u32[]{:S(2)}, u32[]{:S(2)}) collective-permute-start(bf16[80,384]{1,0:T(8,128)(2,1)} %param.9), channel_id=1, source_target_pairs={{1,448},{17,464},{33,480},{49,496},{64,385},{80,401},{96,417},{112... | collective-permute-start | bytes 184328 | tf_op jit(solution)/shard_map/ppermute | solution.py:335
  16.0 3.5 %collective-permute-start = (bf16[256,128]{1,0:T(8,128)(2,1)}, bf16[256,128]{1,0:T(8,128)(2,1)S(1)}, u32[]{:S(2)}, u32[]{:S(2)}) collective-permute-start(bf16[256,128]{1,0:T(8,128)(2,1)} %refs_3_.1), channel_id=1, source_target_pairs={{0,8},{1,9},{2,10},{3,11},{4,12},{5,13},{6,14},{7,15}} | collective-permute-start | bytes 196616 | tf_op jit(solution)/shard_map/ppermute | solution.py:328
  17.3 3.4 %collective-permute-start.1 = (bf16[256,128]{1,0:T(8,128)(2,1)}, bf16[256,128]{1,0:T(8,128)(2,1)S(1)}, u32[]{:S(2)}, u32[]{:S(2)}) collective-permute-start(bf16[256,128]{1,0:T(8,128)(2,1)} %refs_4_.1), channel_id=1, source_target_pairs={{0,8},{1,9},{2,10},{3,11},{4,12},{5,13},{6,14},{7,15}} | collective-permute-start | bytes 196616 | tf_op jit(solution)/shard_map/ppermute | solution.py:328
  20.7 0.8 copy-start.2
  21.5 0.8 copy-start.4
  22.3 0.7 copy-start.6
  39.0 22.5 %collective-permute-start.4 = (bf16[1152,128]{1,0:T(8,128)(2,1)S(1)}, bf16[1152,128]{1,0:T(8,128)(2,1)S(1)}, u32[]{:S(2)}, u32[]{:S(2)}) collective-permute-start(bf16[1152,128]{1,0:T(8,128)(2,1)S(1)} %pad_maximum_fusion.refs_5_), channel_id=1, source_target_pairs={{0,16},{16,32},{32,48},{48,64},{64,80},{80,96},{96,112},{112,0},{1... | collective-permute-start | bytes 884744 | tf_op jit(solution)/shard_map/ppermute | solution.py:360
  40.9 20.6 %collective-permute-start.5 = (bf16[1152,128]{1,0:T(8,128)(2,1)S(1)}, bf16[1152,128]{1,0:T(8,128)(2,1)S(1)}, u32[]{:S(2)}, u32[]{:S(2)}) collective-permute-start(bf16[1152,128]{1,0:T(8,128)(2,1)S(1)} %pad_maximum_fusion.refs_5_), channel_id=1, source_target_pairs={{0,112},{16,0},{32,16},{48,32},{64,48},{80,64},{96,80},{112,96},{1... | collective-permute-start | bytes 884744 | tf_op jit(solution)/shard_map/ppermute | solution.py:361
  54.8 0.8 copy-start.3
  55.6 0.8 copy-start.5
  56.5 1.0 copy-start.7
  57.5 18.1 %copy-start.8 = (bf16[256,640]{1,0:T(8,128)(2,1)S(1)}, bf16[256,640]{1,0:T(8,128)(2,1)}, u32[]{:S(2)}) copy-start(bf16[256,640]{1,0:T(8,128)(2,1)} %refs_1_.9) | copy-start | bytes 983044
  61.6 7.5 %collective-permute-start.9 = (bf16[1152,128]{1,0:T(8,128)(2,1)S(1)}, bf16[1152,128]{1,0:T(8,128)(2,1)S(1)}, u32[]{:S(2)}, u32[]{:S(2)}) collective-permute-start(bf16[1152,128]{1,0:T(8,128)(2,1)S(1)} %collective-permute-done.5.refs_4_), channel_id=1, source_target_pairs={{0,112},{16,0},{32,16},{48,32},{64,48},{80,64},{96,80},{112,96},{1... | collective-permute-start | bytes 884744 | tf_op jit(solution)/shard_map/ppermute | solution.py:368
  64.9 8.7 %collective-permute-start.6 = (bf16[1152,128]{1,0:T(8,128)(2,1)S(1)}, bf16[1152,128]{1,0:T(8,128)(2,1)S(1)}, u32[]{:S(2)}, u32[]{:S(2)}) collective-permute-start(bf16[1152,128]{1,0:T(8,128)(2,1)S(1)} %collective-permute-done.4.refs_3_), channel_id=1, source_target_pairs={{0,16},{16,32},{32,48},{48,64},{64,80},{80,96},{96,112},{112,0},{1... | collective-permute-start | bytes 884744 | tf_op jit(solution)/shard_map/ppermute | solution.py:367
  69.0 14.9 %collective-permute-start.10 = (bf16[1152,128]{1,0:T(8,128)(2,1)S(1)}, bf16[1152,128]{1,0:T(8,128)(2,1)S(1)}, u32[]{:S(2)}, u32[]{:S(2)}) collective-permute-start(bf16[1152,128]{1,0:T(8,128)(2,1)S(1)} %collective-permute-done.9.refs_4_), channel_id=1, source_target_pairs={{0,112},{16,0},{32,16},{48,32},{64,48},{80,64},{96,80},{112,96},{1... | collective-permute-start | bytes 884744 | tf_op jit(solution)/shard_map/ppermute | solution.py:368
  73.6 19.3 %collective-permute-start.7 = (bf16[1152,128]{1,0:T(8,128)(2,1)S(1)}, bf16[1152,128]{1,0:T(8,128)(2,1)S(1)}, u32[]{:S(2)}, u32[]{:S(2)}) collective-permute-start(bf16[1152,128]{1,0:T(8,128)(2,1)S(1)} %collective-permute-done.6.refs_3_), channel_id=1, source_target_pairs={{0,16},{16,32},{32,48},{48,64},{64,80},{80,96},{96,112},{112,0},{1... | collective-permute-start | bytes 884744 | tf_op jit(solution)/shard_map/ppermute | solution.py:367
  84.0 17.6 %collective-permute-start.11 = (bf16[640,128]{1,0:T(8,128)(2,1)S(1)}, bf16[640,128]{1,0:T(8,128)(2,1)S(1)}, u32[]{:S(2)}, u32[]{:S(2)}) collective-permute-start(bf16[640,128]{1,0:T(8,128)(2,1)S(1)} %slice.24), channel_id=1, source_target_pairs={{0,112},{16,0},{32,16},{48,32},{64,48},{80,64},{96,80},{112,96},{1... | collective-permute-start | bytes 491528 | tf_op jit(solution)/shard_map/ppermute | solution.py:377
  92.9 8.6 %collective-permute-start.8 = (bf16[512,128]{1,0:T(8,128)(2,1)S(1)}, bf16[512,128]{1,0:T(8,128)(2,1)S(1)}, u32[]{:S(2)}, u32[]{:S(2)}) collective-permute-start(bf16[512,128]{1,0:T(8,128)(2,1)S(1)} %slice.23), channel_id=1, source_target_pairs={{0,16},{16,32},{32,48},{48,64},{64,80},{80,96},{96,112},{112,0},{1... | collective-permute-start | bytes 393224 | tf_op jit(solution)/shard_map/ppermute | solution.py:376
  103.4 7.3 %collective-permute-start.12 = (f32[5,144,256]{2,1,0:T(8,128)S(1)}, f32[5,144,256]{2,1,0:T(8,128)S(1)}, u32[]{:S(2)}, u32[]{:S(2)}) collective-permute-start(f32[5,144,256]{2,1,0:T(8,128)S(1)} %attend4b.1), channel_id=1, source_target_pairs={{0,8},{8,0},{1,9},{9,1},{2,10},{10,2},{3,11},{11,3},{4,12},{12,4},... | collective-permute-start | bytes 2211848 | tf_op jit(solution)/shard_map/ppermute | solution.py:383
  111.0 17.1 %collective-permute-start.13 = (bf16[256,640]{1,0:T(8,128)(2,1)S(1)}, bf16[256,640]{1,0:T(8,128)(2,1)S(1)}, u32[]{:S(2)}, u32[]{:S(2)}) collective-permute-start(bf16[256,640]{1,0:T(8,128)(2,1)S(1)} %merge.1.refs_0_), channel_id=1, source_target_pairs={{0,4},{2,6},{4,0},{6,2},{1,5},{3,7},{5,1},{7,3},{8,12},{10,14},{12... | collective-permute-start | bytes 983048 | tf_op jit(solution)/shard_map/ppermute | solution.py:390
  118.3 15.2 %collective-permute-start.14 = (bf16[256,640]{1,0:T(8,128)(2,1)S(1)}, bf16[256,640]{1,0:T(8,128)(2,1)S(1)}, u32[]{:S(2)}, u32[]{:S(2)}) collective-permute-start(bf16[256,640]{1,0:T(8,128)(2,1)S(1)} %merge.1.refs_0_), channel_id=1, source_target_pairs={{0,2},{2,4},{4,6},{6,0},{1,3},{3,5},{5,7},{7,1},{8,10},{10,12},{12... | collective-permute-start | bytes 983048 | tf_op jit(solution)/shard_map/ppermute | solution.py:390
  120.5 13.0 %collective-permute-start.15 = (bf16[256,640]{1,0:T(8,128)(2,1)S(1)}, bf16[256,640]{1,0:T(8,128)(2,1)S(1)}, u32[]{:S(2)}, u32[]{:S(2)}) collective-permute-start(bf16[256,640]{1,0:T(8,128)(2,1)S(1)} %merge.1.refs_0_), channel_id=1, source_target_pairs={{0,6},{2,0},{4,2},{6,4},{1,7},{3,1},{5,3},{7,5},{8,14},{10,8},{12,... | collective-permute-start | bytes 983048 | tf_op jit(solution)/shard_map/ppermute | solution.py:390
  125.0 2.1 %copy-start = (bf16[64,240,128]{2,1,0:T(8,128)(2,1)S(1)}, bf16[64,240,128]{2,1,0:T(8,128)(2,1)}, u32[]{:S(2)}) copy-start(bf16[64,240,128]{2,1,0:T(8,128)(2,1)} %all-gather.4.cloned.1.call-done) | copy-start | bytes 11796484
  127.1 6.4 %copy-start.1 = (bf16[64,240,128]{2,1,0:T(8,128)(2,1)S(1)}, bf16[64,240,128]{2,1,0:T(8,128)(2,1)}, u32[]{:S(2)}) copy-start(bf16[64,240,128]{2,1,0:T(8,128)(2,1)} %all-gather.4.cloned.1.call-done) | copy-start | bytes 11796484
  135.3 13.4 %collective-permute-start.16 = (bf16[256,384]{1,0:T(8,128)(2,1)S(1)}, bf16[256,384]{1,0:T(8,128)(2,1)S(1)}, u32[]{:S(2)}, u32[]{:S(2)}) collective-permute-start(bf16[256,384]{1,0:T(8,128)(2,1)S(1)} %far1.1), channel_id=1, source_target_pairs={{0,1},{1,0},{2,3},{3,2},{4,5},{5,4},{6,7},{7,6},{8,9},{9,8},{10,11... | collective-permute-start | bytes 589832 | tf_op jit(solution)/shard_map/ppermute | solution.py:394
Sparse Core Ops, SparseCore 0:
  61.7 48.1 all-gather.3
